TPU v7x, 32 devices: a whole 2x2x4 slice. The times are simulated.
32 devices in a mesh: section: 2 (over core), dp: 4 (over y, x), tensor: 4 (over z).
Axes of the slice: x: 2, y: 2, z: 4, core: 2. Of those that a mesh axis runs over, the one named last changes fastest.
Arguments:
- stack_ends: bfloat16 [2, 8, 1024, 1152], P('section', 'dp', 'tensor'), may hold values from -6 to 6
- cond: bfloat16 [8, 1152], P('dp'), may hold values from -6 to 6
- qkv_weight: bfloat16 [2, 1152, 3, 1152], P('section', 'dp', None, 'tensor'), may hold values from -0.1875 to 0.1875
- out_weight: bfloat16 [2, 1152, 1152], P('section', 'tensor', 'dp'), may hold values from -0.5 to 0.5
- up_weight: bfloat16 [2, 1152, 4608], P('section', 'dp', 'tensor'), may hold values from -0.1875 to 0.1875
- down_weight: bfloat16 [2, 4608, 1152], P('section', 'tensor', 'dp'), may hold values from -0.09375 to 0.09375
- adaln_weight: bfloat16 [2, 1152, 6912], P('section', 'dp', 'tensor'), may hold values from -0.1875 to 0.1875
- qv_bias: bfloat16 [2, 2, 1152], P('section'), may hold values from -2 to 2
- out_bias: bfloat16 [2, 1152], P('section'), may hold values from -2 to 2
- up_bias: bfloat16 [2, 4608], P('section'), may hold values from -2 to 2
- down_bias: bfloat16 [2, 1152], P('section'), may hold values from -2 to 2
- adaln_bias: bfloat16 [2, 6912], P('section'), may hold values from -2 to 2
Outputs:
- result_ends: float32 [2, 8, 1024, 1152], P('section', 'dp', 'tensor')
- cond_grad: float32 [8, 1152], P('dp')
- qkv_grad: float32 [2, 1152, 3, 1152], P('section', 'dp', None, 'tensor')
- out_grad: float32 [2, 1152, 1152], P('section', 'tensor', 'dp')
- up_grad: float32 [2, 1152, 4608], P('section', 'dp', 'tensor')
- down_grad: float32 [2, 4608, 1152], P('section', 'tensor', 'dp')
- adaln_grad: float32 [2, 1152, 6912], P('section', 'dp', 'tensor')
- qv_bias_grad: float32 [2, 2, 1152], P('section')
- out_bias_grad: float32 [2, 1152], P('section')
- up_bias_grad: float32 [2, 4608], P('section')
- down_bias_grad: float32 [2, 1152], P('section')
- adaln_bias_grad: float32 [2, 6912], P('section')
All inputs are finite; a program needn't handle non-finite values.
Results may differ from a plain program's by a relative error of at most 0.019.
Values may be sent and summed in bfloat16 or wider, within the bound.
A program may use at most 256 MiB of HBM per device.

v0:
```python
import math

import jax
import jax.numpy as jnp
from jax import lax
from jax.sharding import PartitionSpec as P

HD = 72
MB = 2


norm_eps = 1e-06


def shifted(value, axis, steps):
    count = lax.axis_size(axis)
    initial, last = (max(0, -steps), min(count, count - steps))
    return lax.ppermute(value, axis, [(source, source + steps) for source in range(initial, last)])


def layer_norm(values):
    centred = values - jnp.mean(values, axis=-1, keepdims=True)
    variance = jnp.mean(centred * centred, axis=-1, keepdims=True)
    return centred * lax.rsqrt(variance + norm_eps)


def norm_back(values, upstream):
    _, pullback = jax.vjp(layer_norm, values)
    return pullback(upstream)[0]


def gelu_tanh(values):
    return jax.nn.gelu(values, approximate=True)


def spread_tokens(values):
    return lax.all_gather(values, "tensor", axis=1, tiled=True)


def collect_tokens(values):
    return lax.psum_scatter(values, "tensor", scatter_dimension=1, tiled=True)


def spread_grads(values):
    return lax.all_gather(values, "tensor", axis=1, tiled=True)


def collect_grads(values):
    return lax.psum_scatter(
        values.astype(jnp.bfloat16), "tensor", scatter_dimension=1, tiled=True
    ).astype(jnp.float32)


def fetch_weights(shards):
    return (
        lax.all_gather(shards[0], "dp", axis=0, tiled=True),
        lax.all_gather(shards[1], "dp", axis=1, tiled=True),
        lax.all_gather(shards[2], "dp", axis=0, tiled=True),
        lax.all_gather(shards[3], "dp", axis=1, tiled=True),
        lax.all_gather(shards[4], "dp", axis=0, tiled=True),
    )


def settle_grads(grads):
    return (
        lax.psum_scatter(
            grads[0].astype(jnp.bfloat16), "dp", scatter_dimension=0, tiled=True
        ).astype(jnp.float32),
        lax.psum_scatter(
            grads[1].astype(jnp.bfloat16), "dp", scatter_dimension=1, tiled=True
        ).astype(jnp.float32),
        lax.psum_scatter(
            grads[2].astype(jnp.bfloat16), "dp", scatter_dimension=0, tiled=True
        ).astype(jnp.float32),
        lax.psum_scatter(
            grads[3].astype(jnp.bfloat16), "dp", scatter_dimension=1, tiled=True
        ).astype(jnp.float32),
        lax.psum_scatter(
            grads[4].astype(jnp.bfloat16), "dp", scatter_dimension=0, tiled=True
        ).astype(jnp.float32),
    )


def split_modulation(modulation, width):
    return [modulation[:, None, part * width : (part + 1) * width] for part in range(6)]


def forward(inputs, silu_part, gathered, biases):
    w_qkv, w_out, w_up, w_down, w_ada = gathered
    b_qv, b_out, b_up, b_down, b_ada = biases
    batch = inputs.shape[0]
    width = inputs.shape[2]
    head_cols = w_qkv.shape[2]
    heads_here = head_cols // HD
    scale_factor = 1.0 / math.sqrt(HD)
    modulation_part = jnp.dot(silu_part, w_ada, preferred_element_type=jnp.float32) + b_ada
    modulation = lax.all_gather(modulation_part, "tensor", axis=1, tiled=True)
    shift_attn, scale_attn, gate_attn, shift_mlp, scale_mlp, gate_mlp = split_modulation(
        modulation, width
    )
    normed = spread_tokens(
        (layer_norm(inputs) * (1.0 + scale_attn) + shift_attn).astype(jnp.bfloat16)
    )
    seq_len = normed.shape[1]
    normed_rows = normed.reshape(batch * seq_len, width)
    projected = jnp.einsum("nd,dcj->ncj", normed_rows, w_qkv, preferred_element_type=jnp.float32)
    queries = (
        (projected[:, 0] + b_qv[0]).astype(jnp.bfloat16).reshape(batch, seq_len, heads_here, HD)
    )
    keys_all = projected[:, 1].astype(jnp.bfloat16).reshape(batch, seq_len, heads_here, HD)
    values_all = (
        (projected[:, 2] + b_qv[1]).astype(jnp.bfloat16).reshape(batch, seq_len, heads_here, HD)
    )
    scores = (
        jnp.einsum("bqhe,bkhe->bhqk", queries, keys_all, preferred_element_type=jnp.float32)
        * scale_factor
    )
    top_score = jnp.max(scores, axis=-1, keepdims=True)
    log_total = top_score + jnp.log(jnp.sum(jnp.exp(scores - top_score), axis=-1, keepdims=True))
    probs_low = jnp.exp(scores - log_total).astype(jnp.bfloat16)
    attended = jnp.einsum(
        "bhqk,bkhe->bqhe", probs_low, values_all, preferred_element_type=jnp.float32
    )
    attended = attended.astype(jnp.bfloat16).reshape(batch * seq_len, head_cols)
    attn_terms = jnp.dot(attended, w_out, preferred_element_type=jnp.float32).reshape(
        batch, seq_len, width
    )
    branch_attn = collect_tokens(attn_terms) + b_out
    middle = inputs + gate_attn * branch_attn
    normed_mlp = spread_tokens(
        (layer_norm(middle) * (1.0 + scale_mlp) + shift_mlp).astype(jnp.bfloat16)
    )
    mlp_rows = normed_mlp.reshape(batch * seq_len, width)
    hidden_pre = jnp.dot(mlp_rows, w_up, preferred_element_type=jnp.float32) + b_up
    hidden = gelu_tanh(hidden_pre).astype(jnp.bfloat16)
    mlp_terms = jnp.dot(hidden, w_down, preferred_element_type=jnp.float32).reshape(
        batch, seq_len, width
    )
    branch_mlp = collect_tokens(mlp_terms) + b_down
    outputs = middle + gate_mlp * branch_mlp
    stored = (
        inputs,
        modulation,
        normed_rows,
        queries,
        keys_all,
        values_all,
        log_total,
        attended,
        branch_attn,
        middle,
        mlp_rows,
        hidden_pre,
        hidden,
        branch_mlp,
        silu_part,
    )
    return (outputs, stored)


def backward(upstream, stored, gathered):
    w_qkv, w_out, w_up, w_down, w_ada = gathered
    (
        inputs,
        modulation,
        normed_rows,
        queries,
        keys_all,
        values_all,
        log_total,
        attended,
        branch_attn,
        middle,
        mlp_rows,
        hidden_pre,
        hidden,
        branch_mlp,
        silu_part,
    ) = stored
    batch = inputs.shape[0]
    width = inputs.shape[2]
    seq_len = queries.shape[1]
    head_cols = w_qkv.shape[2]
    scale_factor = 1.0 / math.sqrt(HD)
    shift_attn, scale_attn, gate_attn, shift_mlp, scale_mlp, gate_mlp = split_modulation(
        modulation, width
    )
    grad_gate_mlp = jnp.sum(upstream * branch_mlp, axis=1)
    grad_branch_mlp = (gate_mlp * upstream).astype(jnp.bfloat16)
    bias_down = jnp.sum(grad_branch_mlp.astype(jnp.float32), axis=(0, 1))
    mlp_grad_rows = spread_grads(grad_branch_mlp).reshape(batch * seq_len, width)
    grad_down = jnp.einsum("nh,nd->hd", hidden, mlp_grad_rows, preferred_element_type=jnp.float32)
    grad_hidden = jnp.einsum("nd,hd->nh", mlp_grad_rows, w_down, preferred_element_type=jnp.float32)
    _, gelu_pull = jax.vjp(gelu_tanh, hidden_pre)
    grad_pre = gelu_pull(grad_hidden)[0].astype(jnp.bfloat16)
    bias_up = jnp.sum(grad_pre.astype(jnp.float32), axis=0)
    grad_up = jnp.einsum("nd,nh->dh", mlp_rows, grad_pre, preferred_element_type=jnp.float32)
    normed_terms = jnp.einsum("nh,dh->nd", grad_pre, w_up, preferred_element_type=jnp.float32)
    grad_normed_mlp = collect_grads(normed_terms.reshape(batch, seq_len, width))
    grad_shift_mlp = jnp.sum(grad_normed_mlp, axis=1)
    grad_scale_mlp = jnp.sum(grad_normed_mlp * layer_norm(middle), axis=1)
    grad_middle = upstream + norm_back(middle, grad_normed_mlp * (1.0 + scale_mlp))
    grad_gate_attn = jnp.sum(grad_middle * branch_attn, axis=1)
    grad_branch_attn = (gate_attn * grad_middle).astype(jnp.bfloat16)
    bias_out = jnp.sum(grad_branch_attn.astype(jnp.float32), axis=(0, 1))
    attn_grad_rows = spread_grads(grad_branch_attn).reshape(batch * seq_len, width)
    grad_out = jnp.einsum("nc,nd->cd", attended, attn_grad_rows, preferred_element_type=jnp.float32)
    grad_attended = jnp.einsum(
        "nd,cd->nc", attn_grad_rows, w_out, preferred_element_type=jnp.float32
    )
    grad_attended = grad_attended.astype(jnp.bfloat16).reshape(queries.shape)
    scores = (
        jnp.einsum("bqhe,bkhe->bhqk", queries, keys_all, preferred_element_type=jnp.float32)
        * scale_factor
    )
    probs = jnp.exp(scores - log_total)
    grad_values = jnp.einsum(
        "bhqk,bqhe->bkhe",
        probs.astype(jnp.bfloat16),
        grad_attended,
        preferred_element_type=jnp.float32,
    ).astype(jnp.bfloat16)
    grad_probs = jnp.einsum(
        "bqhe,bkhe->bhqk", grad_attended, values_all, preferred_element_type=jnp.float32
    )
    grad_scores = (
        probs * (grad_probs - jnp.sum(probs * grad_probs, axis=-1, keepdims=True))
    ).astype(jnp.bfloat16)
    grad_queries = (
        jnp.einsum("bhqk,bkhe->bqhe", grad_scores, keys_all, preferred_element_type=jnp.float32)
        * scale_factor
    ).astype(jnp.bfloat16)
    grad_keys = (
        jnp.einsum("bhqk,bqhe->bkhe", grad_scores, queries, preferred_element_type=jnp.float32)
        * scale_factor
    ).astype(jnp.bfloat16)
    grad_proj = jnp.stack(
        [
            grad_queries.reshape(batch * seq_len, head_cols),
            grad_keys.reshape(batch * seq_len, head_cols),
            grad_values.reshape(batch * seq_len, head_cols),
        ],
        axis=1,
    )
    bias_qv = jnp.stack(
        [
            jnp.sum(grad_proj[:, 0].astype(jnp.float32), axis=0),
            jnp.sum(grad_proj[:, 2].astype(jnp.float32), axis=0),
        ]
    )
    grad_qkv = jnp.einsum("nd,ncj->dcj", normed_rows, grad_proj, preferred_element_type=jnp.float32)
    input_terms = jnp.einsum("ncj,dcj->nd", grad_proj, w_qkv, preferred_element_type=jnp.float32)
    grad_normed = collect_grads(input_terms.reshape(batch, seq_len, width))
    grad_shift_attn = jnp.sum(grad_normed, axis=1)
    grad_scale_attn = jnp.sum(grad_normed * layer_norm(inputs), axis=1)
    grad_inputs = grad_middle + norm_back(inputs, grad_normed * (1.0 + scale_attn))
    mod_terms = jnp.concatenate(
        [
            grad_shift_attn,
            grad_scale_attn,
            grad_gate_attn,
            grad_shift_mlp,
            grad_scale_mlp,
            grad_gate_mlp,
        ],
        axis=1,
    )
    grad_mod = lax.psum_scatter(mod_terms, "tensor", scatter_dimension=1, tiled=True).astype(
        jnp.bfloat16
    )
    bias_ada = jnp.sum(grad_mod.astype(jnp.float32), axis=0)
    grad_ada = jnp.einsum("bd,bm->dm", silu_part, grad_mod, preferred_element_type=jnp.float32)
    grad_silu = jnp.einsum("bm,dm->bd", grad_mod, w_ada, preferred_element_type=jnp.float32)
    return (
        grad_inputs,
        (grad_qkv, grad_out, grad_up, grad_down, grad_ada),
        (bias_qv, bias_out, bias_up, bias_down, bias_ada),
        grad_silu,
    )


def add_trees(first_tree, second_tree):
    if first_tree is None:
        return second_tree
    return jax.tree.map(lambda left, right: left + right, first_tree, second_tree)


def on_device(
    stack_ends,
    cond,
    qkv_weight,
    out_weight,
    up_weight,
    down_weight,
    adaln_weight,
    qv_bias,
    out_bias,
    up_bias,
    down_bias,
    adaln_bias,
):
    section_rank = lax.axis_index("section")
    is_last = section_rank == 1
    tensor_rank = lax.axis_index("tensor")
    width = stack_ends.shape[3]
    split_len = stack_ends.shape[2]
    lat_count = stack_ends.shape[1]
    per_batch = lat_count // MB
    head_cols = qkv_weight.shape[3]
    hidden_cols = up_weight.shape[2]
    mod_cols = adaln_weight.shape[2]
    shards = (qkv_weight[0], out_weight[0], up_weight[0], down_weight[0], adaln_weight[0])
    biases = (
        lax.dynamic_slice_in_dim(
            qv_bias[0].astype(jnp.float32), tensor_rank * head_cols, head_cols, 1
        ),
        out_bias[0].astype(jnp.float32),
        lax.dynamic_slice_in_dim(
            up_bias[0].astype(jnp.float32), tensor_rank * hidden_cols, hidden_cols, 0
        ),
        down_bias[0].astype(jnp.float32),
        lax.dynamic_slice_in_dim(
            adaln_bias[0].astype(jnp.float32), tensor_rank * mod_cols, mod_cols, 0
        ),
    )
    own_rows = stack_ends[0].astype(jnp.float32)
    cond_float = cond.astype(jnp.float32)
    silu_all = jax.nn.silu(cond_float).astype(jnp.bfloat16)
    stored_list = []
    block_outs = []
    received = jnp.zeros((per_batch, split_len, width), jnp.bfloat16)
    for tick_num in range(MB + 1):
        gathered = fetch_weights(shards)
        first_slot = min(tick_num, MB - 1) * per_batch
        source = own_rows[first_slot : first_slot + per_batch]
        inputs = jnp.where(is_last, received.astype(jnp.float32), source)
        batch_index = jnp.clip(tick_num - section_rank, 0, MB - 1)
        silu_part = lax.dynamic_slice_in_dim(silu_all, batch_index * per_batch, per_batch, 0)
        outputs, stored = forward(inputs, silu_part, gathered, biases)
        stored_list.append(stored)
        block_outs.append(outputs)
        received = shifted(outputs.astype(jnp.bfloat16), "section", 1)
    returned = jnp.zeros((per_batch, split_len, width), jnp.bfloat16)
    silu_grads = jnp.zeros((lat_count, width), jnp.float32)
    bias_totals = None
    weight_totals = None
    input_grads = []
    for tick_num in range(MB + 1):
        gathered = fetch_weights(shards)
        if tick_num < MB:
            cot_rows = own_rows[tick_num * per_batch : (tick_num + 1) * per_batch]
        else:
            cot_rows = jnp.zeros((per_batch, split_len, width), jnp.float32)
        upstream = jnp.where(is_last, cot_rows, returned.astype(jnp.float32))
        later = stored_list[min(tick_num + 1, MB)]
        earlier = stored_list[max(tick_num - 1, 0)]
        stored = jax.tree.map(
            lambda first_leaf, second_leaf: jnp.where(is_last, first_leaf, second_leaf),
            later,
            earlier,
        )
        grad_inputs, weight_grads, bias_grads, grad_silu = backward(upstream, stored, gathered)
        returned = shifted(grad_inputs.astype(jnp.bfloat16), "section", -1)
        input_grads.append(grad_inputs)
        batch_start = jnp.clip(tick_num - 1 + section_rank, 0, MB - 1) * per_batch
        current = lax.dynamic_slice_in_dim(silu_grads, batch_start, per_batch, 0)
        silu_grads = lax.dynamic_update_slice_in_dim(
            silu_grads, current + grad_silu, batch_start, 0
        )
        bias_totals = add_trees(bias_totals, bias_grads)
        weight_totals = add_trees(weight_totals, settle_grads(weight_grads))
    outs_section = jnp.concatenate(block_outs[1:], axis=0)
    grads_section = jnp.concatenate(input_grads[1:], axis=0)
    result_ends = jnp.where(is_last, outs_section, grads_section)[None]
    qv_full = lax.dynamic_update_slice_in_dim(
        jnp.zeros((2, width), jnp.float32), bias_totals[0], tensor_rank * head_cols, 1
    )
    up_full = lax.dynamic_update_slice_in_dim(
        jnp.zeros((up_bias.shape[1],), jnp.float32), bias_totals[2], tensor_rank * hidden_cols, 0
    )
    ada_full = lax.dynamic_update_slice_in_dim(
        jnp.zeros((adaln_bias.shape[1],), jnp.float32), bias_totals[4], tensor_rank * mod_cols, 0
    )
    summed = lax.psum(
        (qv_full, bias_totals[1], up_full, bias_totals[3], ada_full), ("dp", "tensor")
    )
    silu_total = lax.psum(silu_grads, ("section", "tensor"))
    _, silu_pull = jax.vjp(jax.nn.silu, cond_float)
    cond_grad = silu_pull(silu_total)[0]
    return (
        result_ends,
        cond_grad,
        weight_totals[0][None],
        weight_totals[1][None],
        weight_totals[2][None],
        weight_totals[3][None],
        weight_totals[4][None],
        summed[0][None],
        summed[1][None],
        summed[2][None],
        summed[3][None],
        summed[4][None],
    )


def solution(mesh):
    in_specs = (
        P("section", "dp", "tensor", None),
        P("dp", None),
        P("section", "dp", None, "tensor"),
        P("section", "tensor", "dp"),
        P("section", "dp", "tensor"),
        P("section", "tensor", "dp"),
        P("section", "dp", "tensor"),
        P("section", None, None),
        P("section", None),
        P("section", None),
        P("section", None),
        P("section", None),
    )
    out_specs = (
        P("section", "dp", "tensor", None),
        P("dp", None),
        P("section", "dp", None, "tensor"),
        P("section", "tensor", "dp"),
        P("section", "dp", "tensor"),
        P("section", "tensor", "dp"),
        P("section", "dp", "tensor"),
        P("section", None, None),
        P("section", None),
        P("section", None),
        P("section", None),
        P("section", None),
    )
    return jax.shard_map(
        on_device, mesh=mesh, in_specs=in_specs, out_specs=out_specs, check_vma=False
    )
```

profile of v0, /device:TPU:0, one launch (start us, length us, event | category | flops | bytes accessed | tf_op | source)
XLA Modules:
  0.0 2877.3 jit_solution(12783400804186691913)
XLA Ops:
  11.4 53.4 %all-gather.49.cloned.1.call-done = bf16[1,1152,1728]{2,1,0:T(8,128)(2,1)} async-done(((bf16[1,288,1728]{2,1,0:T(8,128)(2,1)}), bf16[1,1152,1728]{2,1,0:T(8,128)(2,1)}) %all-gather.49.cloned.1.call-update) | async-done | bytes 3981328 | tf_op jit(solution)/shard_map/all_gather | solution.py:60
  169.0 45.6 %all-gather.25.cloned.1.call-done = bf16[1,1024,1152]{2,1,0:T(8,128)(2,1)} async-done(((bf16[1,256,1152]{2,1,0:T(8,128)(2,1)}), bf16[1,1024,1152]{2,1,0:T(8,128)(2,1)}) %all-gather.25.cloned.1.call-update) | async-done | bytes 2359312 | tf_op jit(solution)/shard_map/all_gather | solution.py:37
  251.7 83.0 %reduce-scatter.43.cloned.1.call-done = f32[1,256,1152]{2,1,0:T(8,128)} async-done(((f32[1,1024,1152]{2,1,0:T(8,128)}), f32[1,256,1152]{2,1,0:T(8,128)}) %reduce-scatter.43.cloned.1.call-update) | async-done | bytes 1179664 | tf_op jit(solution)/shard_map/reduce_scatter | solution.py:41
  377.0 52.7 %all-gather.27.cloned.1.call-done = bf16[1,1024,1152]{2,1,0:T(8,128)(2,1)} async-done(((bf16[1,256,1152]{2,1,0:T(8,128)(2,1)}), bf16[1,1024,1152]{2,1,0:T(8,128)(2,1)}) %all-gather.27.cloned.1.call-update) | async-done | bytes 2359312 | tf_op jit(solution)/shard_map/all_gather | solution.py:37
  480.7 84.7 %reduce-scatter.45.cloned.1.call-done = f32[1,256,1152]{2,1,0:T(8,128)} async-done(((f32[1,1024,1152]{2,1,0:T(8,128)}), f32[1,256,1152]{2,1,0:T(8,128)}) %reduce-scatter.45.cloned.1.call-update) | async-done | bytes 1179664 | tf_op jit(solution)/shard_map/reduce_scatter | solution.py:41
  578.7 51.0 %all-gather.29.cloned.1.call-done = bf16[1,1024,1152]{2,1,0:T(8,128)(2,1)} async-done(((bf16[1,256,1152]{2,1,0:T(8,128)(2,1)}), bf16[1,1024,1152]{2,1,0:T(8,128)(2,1)}) %all-gather.29.cloned.1.call-update) | async-done | bytes 2359312 | tf_op jit(solution)/shard_map/all_gather | solution.py:37
  665.3 83.8 %reduce-scatter.47.cloned.1.call-done = f32[1,256,1152]{2,1,0:T(8,128)} async-done(((f32[1,1024,1152]{2,1,0:T(8,128)}), f32[1,256,1152]{2,1,0:T(8,128)}) %reduce-scatter.47.cloned.1.call-update) | async-done | bytes 1179664 | tf_op jit(solution)/shard_map/reduce_scatter | solution.py:41
  758.9 50.4 %all-gather.31.cloned.1.call-done = bf16[1,1024,1152]{2,1,0:T(8,128)(2,1)} async-done(((bf16[1,256,1152]{2,1,0:T(8,128)(2,1)}), bf16[1,1024,1152]{2,1,0:T(8,128)(2,1)}) %all-gather.31.cloned.1.call-update) | async-done | bytes 2359312 | tf_op jit(solution)/shard_map/all_gather | solution.py:37
  817.3 43.5 %all-gather.37.cloned.1.call-done = bf16[1,1024,1152]{2,1,0:T(8,128)(2,1)} async-done(((bf16[1,256,1152]{2,1,0:T(8,128)(2,1)}), bf16[1,1024,1152]{2,1,0:T(8,128)(2,1)}) %all-gather.37.cloned.1.call-update) | async-done | bytes 2359312 | tf_op jit(solution)/shard_map/all_gather | solution.py:45
  877.1 46.9 %reduce-scatter.55.cloned.1.call-done = bf16[1,256,1152]{2,1,0:T(8,128)(2,1)} async-done(((bf16[1,1024,1152]{2,1,0:T(8,128)(2,1)}), bf16[1,256,1152]{2,1,0:T(8,128)(2,1)}) %reduce-scatter.55.cloned.1.call-update) | async-done | bytes 589840 | tf_op jit(solution)/shard_map/reduce_scatter | solution.py:49
  1072.7 46.6 %reduce-scatter.57.cloned.1.call-done = bf16[1,256,1152]{2,1,0:T(8,128)(2,1)} async-done(((bf16[1,1024,1152]{2,1,0:T(8,128)(2,1)}), bf16[1,256,1152]{2,1,0:T(8,128)(2,1)}) %reduce-scatter.57.cloned.1.call-update) | async-done | bytes 589840 | tf_op jit(solution)/shard_map/reduce_scatter | solution.py:49
  1138.8 49.7 %all-gather.33.cloned.1.call-done = bf16[1,1024,1152]{2,1,0:T(8,128)(2,1)} async-done(((bf16[1,256,1152]{2,1,0:T(8,128)(2,1)}), bf16[1,1024,1152]{2,1,0:T(8,128)(2,1)}) %all-gather.33.cloned.1.call-update) | async-done | bytes 2359312 | tf_op jit(solution)/shard_map/all_gather | solution.py:37
  1224.8 84.0 %reduce-scatter.51.cloned.1.call-done = f32[1,256,1152]{2,1,0:T(8,128)} async-done(((f32[1,1024,1152]{2,1,0:T(8,128)}), f32[1,256,1152]{2,1,0:T(8,128)}) %reduce-scatter.51.cloned.1.call-update) | async-done | bytes 1179664 | tf_op jit(solution)/shard_map/reduce_scatter | solution.py:41
  1319.2 50.4 %all-gather.35.cloned.1.call-done = bf16[1,1024,1152]{2,1,0:T(8,128)(2,1)} async-done(((bf16[1,256,1152]{2,1,0:T(8,128)(2,1)}), bf16[1,1024,1152]{2,1,0:T(8,128)(2,1)}) %all-gather.35.cloned.1.call-update) | async-done | bytes 2359312 | tf_op jit(solution)/shard_map/all_gather | solution.py:37
  1377.8 43.3 %all-gather.41.cloned.1.call-done = bf16[1,1024,1152]{2,1,0:T(8,128)(2,1)} async-done(((bf16[1,256,1152]{2,1,0:T(8,128)(2,1)}), bf16[1,1024,1152]{2,1,0:T(8,128)(2,1)}) %all-gather.41.cloned.1.call-update) | async-done | bytes 2359312 | tf_op jit(solution)/shard_map/all_gather | solution.py:45
  1437.3 46.9 %reduce-scatter.59.cloned.1.call-done = bf16[1,256,1152]{2,1,0:T(8,128)(2,1)} async-done(((bf16[1,1024,1152]{2,1,0:T(8,128)(2,1)}), bf16[1,256,1152]{2,1,0:T(8,128)(2,1)}) %reduce-scatter.59.cloned.1.call-update) | async-done | bytes 589840 | tf_op jit(solution)/shard_map/reduce_scatter | solution.py:49
  1645.9 80.2 %reduce-scatter.53.cloned.1.call-done = f32[1,256,1152]{2,1,0:T(8,128)} async-done(((f32[1,1024,1152]{2,1,0:T(8,128)}), f32[1,256,1152]{2,1,0:T(8,128)}) %reduce-scatter.53.cloned.1.call-update) | async-done | bytes 1179664 | tf_op jit(solution)/shard_map/reduce_scatter | solution.py:41
  1731.6 51.1 %all-gather.45.cloned.1.call-done = bf16[1,1024,1152]{2,1,0:T(8,128)(2,1)} async-done(((bf16[1,256,1152]{2,1,0:T(8,128)(2,1)}), bf16[1,1024,1152]{2,1,0:T(8,128)(2,1)}) %all-gather.45.cloned.1.call-update) | async-done | bytes 2359312 | tf_op jit(solution)/shard_map/all_gather | solution.py:45
  1798.8 47.0 %reduce-scatter.63.cloned.1.call-done = bf16[1,256,1152]{2,1,0:T(8,128)(2,1)} async-done(((bf16[1,1024,1152]{2,1,0:T(8,128)(2,1)}), bf16[1,256,1152]{2,1,0:T(8,128)(2,1)}) %reduce-scatter.63.cloned.1.call-update) | async-done | bytes 589840 | tf_op jit(solution)/shard_map/reduce_scatter | solution.py:49
  2155.5 65.1 %reduce-scatter.95.cloned.1.call-done = f32[1728,1]{1,0:T(8,128)} async-done(((f32[6912,1]{1,0:T(8,128)}), f32[1728,1]{1,0:T(8,128)}) %reduce-scatter.95.cloned.1.call-update) | async-done | bytes 6928
  2497.0 43.2 %reduce-scatter.83.cloned.1.call-done = bf16[1152,288]{0,1:T(8,128)(2,1)} async-done(((bf16[1152,1152]{0,1:T(8,128)(2,1)}), bf16[1152,288]{0,1:T(8,128)(2,1)}) %reduce-scatter.83.cloned.1.call-update) | async-done | bytes 663568 | tf_op jit(solution)/shard_map/reduce_scatter | solution.py:75
  2656.8 43.2 %reduce-scatter.71.cloned.1.call-done = bf16[288,3,288]{2,0,1:T(8,128)(2,1)} async-done(((bf16[1152,3,288]{2,0,1:T(8,128)(2,1)}), bf16[288,3,288]{2,0,1:T(8,128)(2,1)}) %reduce-scatter.71.cloned.1.call-update) | async-done | bytes 497680 | tf_op jit(solution)/shard_map/reduce_scatter | solution.py:66
  2732.2 75.5 %all-reduce.3 = (f32[1,2,1152]{2,1,0:T(2,128)}, f32[1,1152]{1,0:T(1,128)}, f32[1,4608]{1,0:T(1,128)}, f32[1,1152]{1,0:T(1,128)}, f32[1,6912]{1,0:T(1,128)}) all-reduce(f32[1,2,1152]{2,1,0:T(2,128)S(1)} %copy-done.93, f32[1,1152]{1,0:T(1,128)S(1)} %copy-done.112, ...), channel_id=1, replica_groups=mesh['section'=2,'dp'=4,'tensor'=4] {'dp','tensor'}, use_global_device_ids=true, to_apply=%region_100.101 | all-reduce | flops 16128 | bytes 129024 | tf_op jit(solution)/shard_map/psum | solution.py:384
  2811.7 55.4 %reduce-scatter.89.cloned.1.call-done = bf16[288,1728]{1,0:T(8,128)(2,1)} async-done(((bf16[1152,1728]{1,0:T(8,128)(2,1)}), bf16[288,1728]{1,0:T(8,128)(2,1)}) %reduce-scatter.89.cloned.1.call-update) | async-done | bytes 995344 | tf_op jit(solution)/shard_map/reduce_scatter | solution.py:78
  (671 shorter events, 1484.0 us)
Async XLA Ops:
  106.7 228.0 %reduce-scatter.43.cloned.1.call-start = ((), (), s32[]{:S(2)}) async-start(), calls=%async_computation.31 | async-start | bytes 5898240 | tf_op jit(solution)/shard_map/reduce_scatter | solution.py:41
  251.1 178.7 %all-gather.27.cloned.1.call-start = ((), (), s32[]{:S(2)}) async-start(), calls=%async_computation.32 | async-start | bytes 2949120 | tf_op jit(solution)/shard_map/all_gather | solution.py:37
  339.2 226.2 %reduce-scatter.45.cloned.1.call-start = ((), (), s32[]{:S(2)}) async-start(), calls=%async_computation.33 | async-start | bytes 5898240 | tf_op jit(solution)/shard_map/reduce_scatter | solution.py:41
  578.5 170.6 %reduce-scatter.47.cloned.1.call-start = ((), (), s32[]{:S(2)}) async-start(), calls=%async_computation.35 | async-start | bytes 5898240 | tf_op jit(solution)/shard_map/reduce_scatter | solution.py:41
  941.2 178.1 %reduce-scatter.57.cloned.1.call-start = ((), (), s32[]{:S(2)}) async-start(), calls=%async_computation.45 | async-start | bytes 2949120 | tf_op jit(solution)/shard_map/reduce_scatter | solution.py:49
  1138.4 170.5 %reduce-scatter.51.cloned.1.call-start = ((), (), s32[]{:S(2)}) async-start(), calls=%async_computation.39 | async-start | bytes 5898240 | tf_op jit(solution)/shard_map/reduce_scatter | solution.py:41
  1601.5 181.1 %all-gather.45.cloned.1.call-start = ((), (), s32[]{:S(2)}) async-start(), calls=%async_computation.50 | async-start | bytes 2949120 | tf_op jit(solution)/shard_map/all_gather | solution.py:45
  1952.5 171.7 %reduce-scatter.93.cloned.1.call-start = ((), (), s32[]{:S(2)}) async-start(), calls=%async_computation.71 | async-start | bytes 4423680
  2020.2 200.4 %reduce-scatter.95.cloned.1.call-start = ((), (), s32[]{:S(2)}) async-start(), calls=%async_computation.72 | async-start | bytes 4423680
  2023.2 227.9 %reduce-scatter.97.cloned.1.call-start = ((), (), s32[]{:S(2)}) async-start(), calls=%async_computation.73 | async-start | bytes 1105920
  2028.2 253.5 %reduce-scatter.99.cloned.1.call-start = ((), (), s32[]{:S(2)}) async-start(), calls=%async_computation.74 | async-start | bytes 1105920
  2032.1 292.7 %reduce-scatter.73.cloned.1.call-start = ((), (), s32[]{:S(2)}) async-start(), calls=%async_computation.57 | async-start | bytes 3317760 | tf_op jit(solution)/shard_map/reduce_scatter | solution.py:72
  2040.1 327.7 %reduce-scatter.75.cloned.1.call-start = ((), (), s32[]{:S(2)}) async-start(), calls=%async_computation.58 | async-start | bytes 3317760 | tf_op jit(solution)/shard_map/reduce_scatter | solution.py:72
  2047.4 363.5 %reduce-scatter.77.cloned.1.call-start = ((), (), s32[]{:S(2)}) async-start(), calls=%async_computation.59 | async-start | bytes 3317760 | tf_op jit(solution)/shard_map/reduce_scatter | solution.py:72
  2056.2 397.8 %reduce-scatter.79.cloned.1.call-start = ((), (), s32[]{:S(2)}) async-start(), calls=%async_computation.60 | async-start | bytes 3317760 | tf_op jit(solution)/shard_map/reduce_scatter | solution.py:75
  2067.9 429.1 %reduce-scatter.81.cloned.1.call-start = ((), (), s32[]{:S(2)}) async-start(), calls=%async_computation.61 | async-start | bytes 3317760 | tf_op jit(solution)/shard_map/reduce_scatter | solution.py:75
  2079.7 460.5 %reduce-scatter.83.cloned.1.call-start = ((), (), s32[]{:S(2)}) async-start(), calls=%async_computation.62 | async-start | bytes 3317760 | tf_op jit(solution)/shard_map/reduce_scatter | solution.py:75
  2091.5 479.2 %reduce-scatter.101.cloned.1.call-start = ((), (), s32[]{:S(2)}) async-start(), calls=%async_computation.75 | async-start | bytes 1105920
  2096.4 517.3 %reduce-scatter.67.cloned.1.call-start = ((), (), s32[]{:S(2)}) async-start(), calls=%async_computation.54 | async-start | bytes 3317760 | tf_op jit(solution)/shard_map/reduce_scatter | solution.py:66
  2104.9 551.9 %reduce-scatter.69.cloned.1.call-start = ((), (), s32[]{:S(2)}) async-start(), calls=%async_computation.55 | async-start | bytes 3317760 | tf_op jit(solution)/shard_map/reduce_scatter | solution.py:66
  2114.2 585.8 %reduce-scatter.71.cloned.1.call-start = ((), (), s32[]{:S(2)}) async-start(), calls=%async_computation.56 | async-start | bytes 3317760 | tf_op jit(solution)/shard_map/reduce_scatter | solution.py:66
  2123.4 684.9 %reduce-scatter.87.cloned.1.call-start = ((), (), s32[]{:S(2)}) async-start(), calls=%async_computation.64 | async-start | bytes 5160960 | tf_op jit(solution)/shard_map/reduce_scatter | solution.py:78
  2128.1 683.5 %reduce-scatter.85.cloned.1.call-start = ((), (), s32[]{:S(2)}) async-start(), calls=%async_computation.63 | async-start | bytes 5160960 | tf_op jit(solution)/shard_map/reduce_scatter | solution.py:78
  2155.4 711.7 %reduce-scatter.89.cloned.1.call-start = ((), (), s32[]{:S(2)}) async-start(), calls=%async_computation.65 | async-start | bytes 5160960 | tf_op jit(solution)/shard_map/reduce_scatter | solution.py:78
  (168 other events, 7577.7 us)
Sparse Core Ops, SparseCore 0:
  9.9 54.8 all-gather.48
  107.3 54.5 all-gather.50
  164.0 50.4 all-gather.24
  250.6 84.0 reduce-scatter.42
  379.2 50.4 all-gather.26
  480.1 85.2 reduce-scatter.44
  578.6 51.0 all-gather.28
  665.0 84.0 reduce-scatter.46
  758.2 50.9 all-gather.30
  931.5 49.9 all-gather.38
  983.8 84.0 reduce-scatter.48
  1138.5 49.9 all-gather.32
  1224.7 84.0 reduce-scatter.50
  1318.5 50.9 all-gather.34
  1494.1 49.9 all-gather.42
  1641.4 84.7 reduce-scatter.52
  1731.6 50.9 all-gather.44
  1854.4 49.9 all-gather.46
  2016.4 65.8 reduce-scatter.92
  2084.7 66.6 reduce-scatter.90
  2153.9 66.6 reduce-scatter.94
  2703.2 52.3 reduce-scatter.86
  2758.9 52.7 reduce-scatter.84
  2814.9 52.1 reduce-scatter.88
  (23 shorter events, 932.2 us)
where the time goes:
time: 2880 us
  waiting for transfers between devices  2050 us (71%)
  matrix products  413 us (14%)
  other arithmetic  187 us (6%)
  blocking collectives  121 us (4%)
  local copies, waits for them, and re-layouts  82.8 us (3%)
    reduce_scatter x6, waiting for transfers between devices, collect_tokens(): return lax.psum_scatter(values, 'tensor', scatter_dimension=1, tiled=True)  444 us
    all_gather x6, waiting for transfers between devices, spread_tokens(): return lax.all_gather(values, 'tensor', axis=1, tiled=True)  300 us
    reduce_scatter x6, waiting for transfers between devices, collect_grads(): lax.psum_scatter(values.astype(jnp.bfloat16), 'tensor', scatter_dimension...  263 us
    all_gather x6, waiting for transfers between devices, spread_grads(): return lax.all_gather(values, 'tensor', axis=1, tiled=True)  250 us
    unnamed x54, waiting for transfers between devices  205 us
    reduce_scatter x3, waiting for transfers between devices, settle_grads(): lax.psum_scatter(grads[3].astype(jnp.bfloat16), 'dp', scatter_dimension=1...  127 us
    reduce_scatter x3, waiting for transfers between devices, settle_grads(): lax.psum_scatter(grads[0].astype(jnp.bfloat16), 'dp', scatter_dimension=0...  125 us
    reduce_scatter x3, waiting for transfers between devices, settle_grads(): lax.psum_scatter(grads[2].astype(jnp.bfloat16), 'dp', scatter_dimension=0...  125 us
  transfers between devices with their start and end apart: 51, of which 47 were waited for; matrix products, arithmetic and copies ran while one was open for 11% of the time, Pallas kernels for 0%

commit v1 on v0

v1 whole, which is shorter than its diff:
```python
import math

import jax
import jax.numpy as jnp
from jax import lax
from jax.sharding import PartitionSpec as P

HD = 72
norm_eps = 1e-06
SWAP = [(0, 1), (1, 0)]
SCALE = 1.0 / math.sqrt(HD)


def norm_parts(values):
    centred = values - jnp.mean(values, axis=-1, keepdims=True)
    inverse = lax.rsqrt(jnp.mean(centred * centred, axis=-1, keepdims=True) + norm_eps)
    return centred * inverse, inverse


def norm_back(normal, inverse, grad):
    pulled = grad - jnp.mean(grad, axis=-1, keepdims=True)
    return (pulled - normal * jnp.mean(grad * normal, axis=-1, keepdims=True)) * inverse


def gelu_tanh(values):
    return jax.nn.gelu(values, approximate=True)


def spread(values):
    return lax.all_gather(values, "tensor", axis=0, tiled=True)


def collect(values):
    return lax.psum_scatter(
        values.astype(jnp.bfloat16), "tensor", scatter_dimension=0, tiled=True
    ).astype(jnp.float32)


def mm(left, right, left_dim, right_dim):
    return lax.dot_general(
        left, right, (((left_dim,), (right_dim,)), ((), ())), preferred_element_type=jnp.float32
    )


def heads_first(rows):
    return rows.reshape(rows.shape[0], -1, HD).transpose(1, 0, 2)


def heads_side(heads):
    return heads.transpose(1, 0, 2).reshape(heads.shape[1], -1)


def forward(inputs, modulation, w_attn, w_mlp, biases):
    b_qkv, b_out, b_up, b_down = biases
    shift_attn, scale_attn, gate_attn, shift_mlp, scale_mlp, gate_mlp = modulation
    cols = w_attn.shape[1] // 4
    units = w_mlp.shape[1] // 2
    norm_in, inv_in = norm_parts(inputs)
    normed = spread((norm_in * (1.0 + scale_attn) + shift_attn).astype(jnp.bfloat16))
    projected = (mm(normed, w_attn[:, : 3 * cols], 1, 0) + b_qkv).astype(jnp.bfloat16)
    queries, keys, values = [
        heads_first(projected[:, part * cols : (part + 1) * cols]) for part in range(3)
    ]
    scores = jnp.einsum("hqe,hke->hqk", queries, keys, preferred_element_type=jnp.float32) * SCALE
    probs = jax.nn.softmax(scores, axis=-1).astype(jnp.bfloat16)
    attended = jnp.einsum("hqk,hke->hqe", probs, values, preferred_element_type=jnp.float32)
    attended = attended.astype(jnp.bfloat16)
    attended_rows = heads_side(attended)
    branch_attn = collect(mm(attended_rows, w_attn[:, 3 * cols :], 1, 1)) + b_out
    middle = inputs + gate_attn * branch_attn
    norm_mid, inv_mid = norm_parts(middle)
    normed_mlp = spread((norm_mid * (1.0 + scale_mlp) + shift_mlp).astype(jnp.bfloat16))
    hidden_pre = mm(normed_mlp, w_mlp[:, :units], 1, 0) + b_up
    hidden = gelu_tanh(hidden_pre).astype(jnp.bfloat16)
    branch_mlp = collect(mm(hidden, w_mlp[:, units:], 1, 1)) + b_down
    outputs = middle + gate_mlp * branch_mlp
    stored = (
        norm_in, inv_in, normed, queries, keys, values, probs, attended, attended_rows,
        branch_attn, norm_mid, inv_mid, normed_mlp, hidden_pre, hidden, branch_mlp,
    )
    return outputs, stored


def backward(upstream, stored, modulation, w_attn, w_mlp):
    (
        norm_in, inv_in, normed, queries, keys, values, probs, attended, attended_rows,
        branch_attn, norm_mid, inv_mid, normed_mlp, hidden_pre, hidden, branch_mlp,
    ) = stored
    shift_attn, scale_attn, gate_attn, shift_mlp, scale_mlp, gate_mlp = modulation
    cols = w_attn.shape[1] // 4
    units = w_mlp.shape[1] // 2
    grad_gate_mlp = jnp.sum(upstream * branch_mlp, axis=0)
    grad_branch = (gate_mlp * upstream).astype(jnp.bfloat16)
    bias_down = jnp.sum(grad_branch.astype(jnp.float32), axis=0)
    grad_rows = spread(grad_branch)
    grad_hidden = mm(grad_rows, w_mlp[:, units:], 1, 0)
    _, gelu_pull = jax.vjp(gelu_tanh, hidden_pre)
    grad_pre = gelu_pull(grad_hidden)[0].astype(jnp.bfloat16)
    grad_normed = collect(mm(grad_pre, w_mlp[:, :units], 1, 1))
    bias_up = jnp.sum(grad_pre.astype(jnp.float32), axis=0)
    mlp_grads = jnp.concatenate(
        [
            mm(normed_mlp, grad_pre, 0, 0).astype(jnp.bfloat16),
            mm(grad_rows, hidden, 0, 0).astype(jnp.bfloat16),
        ],
        axis=1,
    )
    grad_shift_mlp = jnp.sum(grad_normed, axis=0)
    grad_scale_mlp = jnp.sum(grad_normed * norm_mid, axis=0)
    grad_middle = upstream + norm_back(norm_mid, inv_mid, grad_normed * (1.0 + scale_mlp))
    grad_gate_attn = jnp.sum(grad_middle * branch_attn, axis=0)
    grad_branch = (gate_attn * grad_middle).astype(jnp.bfloat16)
    bias_out = jnp.sum(grad_branch.astype(jnp.float32), axis=0)
    grad_rows = spread(grad_branch)
    grad_attended = heads_first(mm(grad_rows, w_attn[:, 3 * cols :], 1, 0).astype(jnp.bfloat16))
    row_sums = jnp.sum(
        grad_attended.astype(jnp.float32) * attended.astype(jnp.float32), axis=-1, keepdims=True
    )
    grad_probs = jnp.einsum(
        "hqe,hke->hqk", grad_attended, values, preferred_element_type=jnp.float32
    )
    grad_scores = (probs.astype(jnp.float32) * (grad_probs - row_sums)).astype(jnp.bfloat16)
    grad_values = jnp.einsum(
        "hqk,hqe->hke", probs, grad_attended, preferred_element_type=jnp.float32
    )
    grad_queries = SCALE * jnp.einsum(
        "hqk,hke->hqe", grad_scores, keys, preferred_element_type=jnp.float32
    )
    grad_keys = SCALE * jnp.einsum(
        "hqk,hqe->hke", grad_scores, queries, preferred_element_type=jnp.float32
    )
    grad_proj = jnp.concatenate(
        [
            heads_side(member.astype(jnp.bfloat16))
            for member in (grad_queries, grad_keys, grad_values)
        ],
        axis=1,
    )
    grad_normed = collect(mm(grad_proj, w_attn[:, : 3 * cols], 1, 1))
    bias_qkv = jnp.sum(grad_proj.astype(jnp.float32), axis=0)
    attn_grads = jnp.concatenate(
        [
            mm(normed, grad_proj, 0, 0).astype(jnp.bfloat16),
            mm(grad_rows, attended_rows, 0, 0).astype(jnp.bfloat16),
        ],
        axis=1,
    )
    grad_shift_attn = jnp.sum(grad_normed, axis=0)
    grad_scale_attn = jnp.sum(grad_normed * norm_in, axis=0)
    grad_inputs = grad_middle + norm_back(norm_in, inv_in, grad_normed * (1.0 + scale_attn))
    mod_terms = jnp.concatenate(
        [
            grad_shift_attn, grad_scale_attn, grad_gate_attn,
            grad_shift_mlp, grad_scale_mlp, grad_gate_mlp,
        ]
    )
    bias_grads = (bias_qkv[:cols], bias_qkv[2 * cols :], bias_out, bias_up, bias_down)
    return grad_inputs, attn_grads, mlp_grads, bias_grads, mod_terms


def on_device(
    stack_ends,
    cond,
    qkv_weight,
    out_weight,
    up_weight,
    down_weight,
    adaln_weight,
    qv_bias,
    out_bias,
    up_bias,
    down_bias,
    adaln_bias,
):
    section_rank = lax.axis_index("section")
    tensor_rank = lax.axis_index("tensor")
    dp_rank = lax.axis_index("dp")
    is_first = section_rank == 0
    width = stack_ends.shape[3]
    depth = qkv_weight.shape[1]
    cols = qkv_weight.shape[3]
    units = up_weight.shape[2]
    mod_cols = adaln_weight.shape[2]
    lat_here = cond.shape[0]
    lat_all = lat_here * lax.axis_size("dp")

    def swap(value):
        return lax.ppermute(value, "section", SWAP)

    def by_block(own, other):
        return (jnp.where(is_first, own, other), jnp.where(is_first, other, own))

    own_ends = stack_ends[0]
    mine = lax.dynamic_index_in_dim(own_ends, section_rank, 0, keepdims=False)
    theirs = swap(lax.dynamic_index_in_dim(own_ends, 1 - section_rank, 0, keepdims=False))
    inputs, cotangent = by_block(mine, theirs)

    cond_all = lax.all_gather(cond, "dp", axis=0, tiled=True).astype(jnp.float32)
    silu_all = jax.nn.silu(cond_all).astype(jnp.bfloat16)
    silu_rows = lax.dynamic_slice_in_dim(silu_all, dp_rank * depth, depth, 1)
    mod_part = lax.psum_scatter(
        mm(silu_rows, adaln_weight[0], 1, 0), "dp", scatter_dimension=0, tiled=True
    )
    mod_all = lax.all_gather(mod_part, ("section", "tensor"), axis=0)
    mod_own = lax.dynamic_index_in_dim(mod_all, section_rank, 1, keepdims=False)
    mod_own = mod_own.reshape(2, -1)

    attn_own = lax.all_gather(
        jnp.concatenate([qkv_weight[0].reshape(depth, 3 * cols), out_weight[0].T], axis=1),
        "dp", axis=0, tiled=True,
    )
    attn_blocks = by_block(attn_own, swap(attn_own))
    mlp_own = lax.all_gather(
        jnp.concatenate([up_weight[0], down_weight[0].T], axis=1), "dp", axis=0, tiled=True
    )
    mlp_blocks = by_block(mlp_own, swap(mlp_own))

    bias_flat = jnp.concatenate(
        [qv_bias[0].reshape(-1), out_bias[0], up_bias[0], down_bias[0], adaln_bias[0]]
    )
    bias_blocks = by_block(bias_flat, swap(bias_flat))
    sizes = (width, width, width, up_bias.shape[1], width, adaln_bias.shape[1])
    marks = [0]
    for size in sizes:
        marks.append(marks[-1] + size)

    modulations = []
    biases = []
    for block in range(2):
        parts = [
            bias_blocks[block][marks[k] : marks[k + 1]].astype(jnp.float32) for k in range(6)
        ]

        def cut(vector, size):
            return lax.dynamic_slice_in_dim(vector, tensor_rank * size, size, 0)

        b_qkv = jnp.concatenate(
            [cut(parts[0], cols), jnp.zeros((cols,), jnp.float32), cut(parts[1], cols)]
        )
        biases.append((b_qkv, parts[2], cut(parts[3], units), parts[4]))
        whole = (mod_own[block] + parts[5]).reshape(6, 1, width)
        modulations.append([whole[k] for k in range(6)])

    boundary, stored_first = forward(
        inputs.astype(jnp.float32), modulations[0], attn_blocks[0], mlp_blocks[0], biases[0]
    )
    boundary = boundary.astype(jnp.bfloat16).astype(jnp.float32)
    outputs, stored_last = forward(
        boundary, modulations[1], attn_blocks[1], mlp_blocks[1], biases[1]
    )
    back_last = backward(
        cotangent.astype(jnp.float32), stored_last, modulations[1], attn_blocks[1], mlp_blocks[1]
    )
    upstream = back_last[0].astype(jnp.bfloat16).astype(jnp.float32)
    back_first = backward(
        upstream, stored_first, modulations[0], attn_blocks[0], mlp_blocks[0]
    )
    backs = (back_first, back_last)

    def settle(which):
        kept = jnp.where(is_first, backs[0][which], backs[1][which])
        sent = swap(jnp.where(is_first, backs[1][which], backs[0][which]))
        total = (kept.astype(jnp.float32) + sent.astype(jnp.float32)).astype(jnp.bfloat16)
        return lax.psum_scatter(total, "dp", scatter_dimension=0, tiled=True).astype(jnp.float32)

    mlp_total = settle(2)
    attn_total = settle(1)

    first_end, last_end = back_first[0], outputs
    kept = jnp.where(is_first, first_end, last_end)
    sent = swap(jnp.where(is_first, last_end, first_end))
    result_ends = jnp.stack(by_block(kept, sent))[None]

    mod_terms = lax.psum_scatter(
        jnp.stack([backs[0][4], backs[1][4]]), "tensor", scatter_dimension=1, tiled=True
    )
    mod_grads = lax.all_gather(mod_terms, ("dp", "section"), axis=0)
    mod_grads = lax.dynamic_index_in_dim(mod_grads, section_rank, 1, keepdims=False)
    mod_grads = mod_grads.astype(jnp.bfloat16)
    grad_ada = mm(silu_rows, mod_grads, 0, 0)
    bias_ada = jnp.sum(mod_grads.astype(jnp.float32), axis=0)
    grad_silu = mm(mod_grads, adaln_weight[0], 1, 1)

    def place(vector, size, rank):
        return lax.dynamic_update_slice_in_dim(
            jnp.zeros((size,), jnp.float32), vector, rank * vector.shape[0], 0
        )

    pieces = []
    for block in range(2):
        bias_q, bias_v, bias_out, bias_up, bias_down = backs[block][3]
        share = jnp.where((section_rank == block) & (dp_rank == 0), bias_ada, 0.0)
        pieces += [
            place(bias_q, width, tensor_rank),
            place(bias_v, width, tensor_rank),
            bias_out,
            place(bias_up, sizes[3], tensor_rank),
            bias_down,
            place(share, sizes[5], tensor_rank),
        ]
    pieces.append(
        lax.dynamic_update_slice_in_dim(
            jnp.zeros((lat_all, width), jnp.float32), grad_silu, dp_rank * depth, 1
        ).reshape(-1)
    )
    summed = lax.psum(jnp.concatenate(pieces), ("section", "dp", "tensor"))
    per_block = marks[-1]
    bias_sums = jnp.where(is_first, summed[:per_block], summed[per_block : 2 * per_block])
    silu_total = summed[2 * per_block :].reshape(lat_all, width)
    silu_total = lax.dynamic_slice_in_dim(silu_total, dp_rank * lat_here, lat_here, 0)
    _, silu_pull = jax.vjp(jax.nn.silu, cond.astype(jnp.float32))
    cond_grad = silu_pull(silu_total)[0]
    return (
        result_ends,
        cond_grad,
        attn_total[:, : 3 * cols].reshape(1, depth, 3, cols),
        attn_total[:, 3 * cols :].T[None],
        mlp_total[:, :units][None],
        mlp_total[:, units:].T[None],
        grad_ada[None],
        bias_sums[: marks[2]].reshape(1, 2, width),
        bias_sums[marks[2] : marks[3]][None],
        bias_sums[marks[3] : marks[4]][None],
        bias_sums[marks[4] : marks[5]][None],
        bias_sums[marks[5] :][None],
    )


def solution(mesh):
    in_specs = (
        P("section", "dp", "tensor", None),
        P("dp", None),
        P("section", "dp", None, "tensor"),
        P("section", "tensor", "dp"),
        P("section", "dp", "tensor"),
        P("section", "tensor", "dp"),
        P("section", "dp", "tensor"),
        P("section", None, None),
        P("section", None),
        P("section", None),
        P("section", None),
        P("section", None),
    )
    out_specs = (
        P("section", "dp", "tensor", None),
        P("dp", None),
        P("section", "dp", None, "tensor"),
        P("section", "tensor", "dp"),
        P("section", "dp", "tensor"),
        P("section", "tensor", "dp"),
        P("section", "dp", "tensor"),
        P("section", None, None),
        P("section", None),
        P("section", None),
        P("section", None),
        P("section", None),
    )
    return jax.shard_map(
        on_device, mesh=mesh, in_specs=in_specs, out_specs=out_specs, check_vma=False
    )
```

time: 2880 us -> 1430 us (0.50)
  waiting for transfers between devices: 2050 us -> 967 us
  matrix products: 413 us -> 180 us
  other arithmetic: 187 us -> 102 us
  blocking collectives: 121 us -> 60.8 us
    reduce_scatter x24 -> x8, waiting for transfers between devices: 1140 us -> 329 us  [collect(): lax.psum_scatter(values.astype(jnp.bfloat16), 'tensor', scatter_dimension...]
    all_gather x16 -> x10, waiting for transfers between devices: 694 us -> 401 us  [the longest x8 366 us: spread(): return lax.all_gather(values, 'tensor', axis=0, tiled=True)]
    dot_general x63 -> x37, matrix products: 413 us -> 160 us  [the longest x27 120 us: mm(): lax.dot_general(left, right, (((left_dim,), (right_dim,)), ((), ())), pre...]
    psum x2 -> x0, blocking collectives: 93.3 us -> none  [the longest x1 75.5 us: on_device(): lax.psum((qv_full, bias_totals[1], up_full, bias_totals[3], ada_full), ('...]
    reduce_sum x38 -> x22, other arithmetic: 105 us -> 29.7 us  [the longest x3 4.45 us: norm_parts(): centred = values - jnp.mean(values, axis=-1, keepdims=True)]
    psum x0 -> x1, waiting for transfers between devices: none -> 70.9 us  [on_device(): summed = lax.psum(jnp.concatenate(pieces), ('section', 'dp', 'tensor'))]
    unnamed x54 -> x25, waiting for transfers between devices: 205 us -> 158 us
    unnamed x315 -> x250, local copies, waits for them, and re-layouts: 65.2 us -> 60 us
  transfers between devices with their start and end apart: 51 -> 29, of which waited for: 47 -> 23; matrix products, arithmetic and copies ran while one was open for 11% -> 14% of each run, Pallas kernels for 0% -> 0%
where the time goes in v1:
time: 1430 us; the launch traced here: 1420 us
  waiting for transfers between devices  967 us (68%)
  matrix products  180 us (13%)
  other arithmetic  102 us (7%)
  local copies, waits for them, and re-layouts  91.6 us (6%)
  blocking collectives  60.8 us (4%)
  between operations  17 us (1%)
    all_gather x8, waiting for transfers between devices, spread(): return lax.all_gather(values, 'tensor', axis=0, tiled=True)  366 us
    reduce_scatter x8, waiting for transfers between devices, collect(): lax.psum_scatter(values.astype(jnp.bfloat16), 'tensor', scatter_dimension...  329 us
    unnamed x25, waiting for transfers between devices  158 us
    dot_general x27, matrix products, mm(): lax.dot_general(left, right, (((left_dim,), (right_dim,)), ((), ())), pre...  120 us
    psum x1, waiting for transfers between devices, on_device(): summed = lax.psum(jnp.concatenate(pieces), ('section', 'dp', 'tensor'))  70.9 us
    unnamed x250, local copies, waits for them, and re-layouts  60 us
    all_gather x1, waiting for transfers between devices, on_device(): lax.all_gather(jnp.concatenate([up_weight[0], down_weight[0].T], axis=1),...  34.7 us
  transfers between devices with their start and end apart: 29, of which 23 were waited for; matrix products, arithmetic and copies ran while one was open for 14% of the time, Pallas kernels for 0%

profile of v1, /device:TPU:0, one launch (start us, length us, event | category | flops | bytes accessed | tf_op | source)
XLA Modules:
  0.0 1422.8 jit_solution(9808158392047033413)
XLA Ops:
  19.5 9.8 all-gather.2
  30.9 17.4 %all-reduce = f32[8,1728]{1,0:T(8,128)S(1)} all-reduce(f32[8,1728]{1,0:T(8,128)S(1)} %fusion.97), channel_id=4, replica_groups=mesh['section'=2,'dp'=4,'tensor'=4] {'dp'}, use_global_device_ids=true, to_apply=%region_0.1.clone | all-reduce | flops 13824 | bytes 110592
  48.3 24.3 %all-gather.3 = f32[8,2,1728]{2,1,0:T(2,128)S(1)} all-gather(f32[1,2,1728]{2,1,0:T(2,128)S(1)} %dynamic-slice_bitcast_fusion.1), channel_id=2, replica_groups=mesh['section'=2,'dp'=4,'tensor'=4] {'section','tensor'}, dimensions={0}, use_global_device_ids=true | all-gather | bytes 124416 | tf_op jit(solution)/shard_map/all_gather | solution.py:204
  96.0 34.1 %all-gather.20.cloned.1.call-done = bf16[1024,1152]{1,0:T(8,128)(2,1)} async-done(((bf16[256,1152]{1,0:T(8,128)(2,1)}), bf16[1024,1152]{1,0:T(8,128)(2,1)}) %all-gather.20.cloned.1.call-update) | async-done | bytes 2359312 | tf_op jit(solution)/shard_map/all_gather | solution.py:30
  158.6 34.7 %all-gather.18.cloned.1.call-done = bf16[1152,2304]{1,0:T(8,128)(2,1)} async-done(((bf16[288,2304]{1,0:T(8,128)(2,1)}), bf16[1152,2304]{1,0:T(8,128)(2,1)}) %all-gather.18.cloned.1.call-update) | async-done | bytes 5308432 | tf_op jit(solution)/shard_map/all_gather | solution.py:213
  201.9 42.3 %reduce-scatter.18.cloned.1.call-done = bf16[256,1152]{1,0:T(8,128)(2,1)} async-done(((bf16[1024,1152]{1,0:T(8,128)(2,1)}), bf16[256,1152]{1,0:T(8,128)(2,1)}) %reduce-scatter.18.cloned.1.call-update) | async-done | bytes 589840 | tf_op jit(solution)/shard_map/reduce_scatter | solution.py:34
  257.9 40.6 %all-gather.24.cloned.1.call-done = bf16[1024,1152]{1,0:T(8,128)(2,1)} async-done(((bf16[256,1152]{1,0:T(8,128)(2,1)}), bf16[1024,1152]{1,0:T(8,128)(2,1)}) %all-gather.24.cloned.1.call-update) | async-done | bytes 2359312 | tf_op jit(solution)/shard_map/all_gather | solution.py:30
  312.3 47.0 %reduce-scatter.20.cloned.1.call-done = bf16[256,1152]{1,0:T(8,128)(2,1)} async-done(((bf16[1024,1152]{1,0:T(8,128)(2,1)}), bf16[256,1152]{1,0:T(8,128)(2,1)}) %reduce-scatter.20.cloned.1.call-update) | async-done | bytes 589840 | tf_op jit(solution)/shard_map/reduce_scatter | solution.py:34
  362.6 49.9 %all-gather.26.cloned.1.call-done = bf16[1024,1152]{1,0:T(8,128)(2,1)} async-done(((bf16[256,1152]{1,0:T(8,128)(2,1)}), bf16[1024,1152]{1,0:T(8,128)(2,1)}) %all-gather.26.cloned.1.call-update) | async-done | bytes 2359312 | tf_op jit(solution)/shard_map/all_gather | solution.py:30
  418.3 10.1 fusion.134
  443.6 46.9 %reduce-scatter.22.cloned.1.call-done = bf16[256,1152]{1,0:T(8,128)(2,1)} async-done(((bf16[1024,1152]{1,0:T(8,128)(2,1)}), bf16[256,1152]{1,0:T(8,128)(2,1)}) %reduce-scatter.22.cloned.1.call-update) | async-done | bytes 589840 | tf_op jit(solution)/shard_map/reduce_scatter | solution.py:34
  495.7 49.1 %all-gather.28.cloned.1.call-done = bf16[1024,1152]{1,0:T(8,128)(2,1)} async-done(((bf16[256,1152]{1,0:T(8,128)(2,1)}), bf16[1024,1152]{1,0:T(8,128)(2,1)}) %all-gather.28.cloned.1.call-update) | async-done | bytes 2359312 | tf_op jit(solution)/shard_map/all_gather | solution.py:30
  553.1 43.1 %all-gather.16.cloned.1.call-done = bf16[1024,1152]{1,0:T(8,128)(2,1)} async-done(((bf16[256,1152]{1,0:T(8,128)(2,1)}), bf16[1024,1152]{1,0:T(8,128)(2,1)}) %all-gather.16.cloned.1.call-update) | async-done | bytes 2359312 | tf_op jit(solution)/shard_map/all_gather | solution.py:30
  612.9 47.0 %reduce-scatter.24.cloned.1.call-done = bf16[256,1152]{1,0:T(8,128)(2,1)} async-done(((bf16[1024,1152]{1,0:T(8,128)(2,1)}), bf16[256,1152]{1,0:T(8,128)(2,1)}) %reduce-scatter.24.cloned.1.call-update) | async-done | bytes 589840 | tf_op jit(solution)/shard_map/reduce_scatter | solution.py:34
  665.4 49.6 %all-gather.30.cloned.1.call-done = bf16[1024,1152]{1,0:T(8,128)(2,1)} async-done(((bf16[256,1152]{1,0:T(8,128)(2,1)}), bf16[1024,1152]{1,0:T(8,128)(2,1)}) %all-gather.30.cloned.1.call-update) | async-done | bytes 2359312 | tf_op jit(solution)/shard_map/all_gather | solution.py:30
  741.9 47.0 %reduce-scatter.26.cloned.1.call-done = bf16[256,1152]{1,0:T(8,128)(2,1)} async-done(((bf16[1024,1152]{1,0:T(8,128)(2,1)}), bf16[256,1152]{1,0:T(8,128)(2,1)}) %reduce-scatter.26.cloned.1.call-update) | async-done | bytes 589840 | tf_op jit(solution)/shard_map/reduce_scatter | solution.py:34
  795.7 49.9 %all-gather.32.cloned.1.call-done = bf16[1024,1152]{1,0:T(8,128)(2,1)} async-done(((bf16[256,1152]{1,0:T(8,128)(2,1)}), bf16[1024,1152]{1,0:T(8,128)(2,1)}) %all-gather.32.cloned.1.call-update) | async-done | bytes 2359312 | tf_op jit(solution)/shard_map/all_gather | solution.py:30
  862.2 47.0 %reduce-scatter.28.cloned.1.call-done = bf16[256,1152]{1,0:T(8,128)(2,1)} async-done(((bf16[1024,1152]{1,0:T(8,128)(2,1)}), bf16[256,1152]{1,0:T(8,128)(2,1)}) %reduce-scatter.28.cloned.1.call-update) | async-done | bytes 589840 | tf_op jit(solution)/shard_map/reduce_scatter | solution.py:34
  915.3 49.9 %all-gather.34.cloned.1.call-done = bf16[1024,1152]{1,0:T(8,128)(2,1)} async-done(((bf16[256,1152]{1,0:T(8,128)(2,1)}), bf16[1024,1152]{1,0:T(8,128)(2,1)}) %all-gather.34.cloned.1.call-update) | async-done | bytes 2359312 | tf_op jit(solution)/shard_map/all_gather | solution.py:30
  1040.7 48.6 %reduce-scatter.32.cloned.1.call-done = bf16[256,1152]{1,0:T(8,128)(2,1)} async-done(((bf16[1024,1152]{1,0:T(8,128)(2,1)}), bf16[256,1152]{1,0:T(8,128)(2,1)}) %reduce-scatter.32.cloned.1.call-update) | async-done | bytes 589840 | tf_op jit(solution)/shard_map/reduce_scatter | solution.py:34
  1097.0 65.1 %reduce-scatter.34.cloned.1.call-done = f32[1728,2]{1,0:T(8,128)} async-done(((f32[6912,2]{1,0:T(8,128)}), f32[1728,2]{1,0:T(8,128)}) %reduce-scatter.34.cloned.1.call-update) | async-done | bytes 13840
  1226.1 70.9 %all-reduce.3.cloned.1.call-done = f32[41472]{0:T(1024)} async-done(((f32[41472]{0:T(1024)}), f32[41472]{0:T(1024)}) %all-reduce.3.cloned.1.call-update) | async-done | bytes 165904 | tf_op jit(solution)/shard_map/psum | solution.py:306
  1306.2 57.9 %reduce-scatter.38.cloned.1.call-done = bf16[288,2304]{1,0:T(8,128)(2,1)} async-done(((bf16[1152,2304]{1,0:T(8,128)(2,1)}), bf16[288,2304]{1,0:T(8,128)(2,1)}) %reduce-scatter.38.cloned.1.call-update) | async-done | bytes 1327120
  1372.4 34.6 %reduce-scatter.36.cloned.1.call-done = bf16[288,1152]{1,0:T(8,128)(2,1)} async-done(((bf16[1152,1152]{1,0:T(8,128)(2,1)}), bf16[288,1152]{1,0:T(8,128)(2,1)}) %reduce-scatter.36.cloned.1.call-update) | async-done | bytes 663568
  (485 shorter events, 389.1 us)
Async XLA Ops:
  7.2 72.7 %all-gather.22.cloned.1.call-start = ((), (), s32[]{:S(2)}) async-start(), calls=%async_computation.14 | async-start | bytes 3317760 | tf_op jit(solution)/shard_map/all_gather | solution.py:208
  11.0 119.1 %all-gather.20.cloned.1.call-start = ((), (), s32[]{:S(2)}) async-start(), calls=%async_computation.13 | async-start | bytes 2949120 | tf_op jit(solution)/shard_map/all_gather | solution.py:30
  79.9 113.5 %all-gather.18.cloned.1.call-start = ((), (), s32[]{:S(2)}) async-start(), calls=%async_computation.12 | async-start | bytes 6635520 | tf_op jit(solution)/shard_map/all_gather | solution.py:213
  86.7 157.4 %reduce-scatter.18.cloned.1.call-start = ((), (), s32[]{:S(2)}) async-start(), calls=%async_computation.15 | async-start | bytes 2949120 | tf_op jit(solution)/shard_map/reduce_scatter | solution.py:34
  158.6 139.9 %all-gather.24.cloned.1.call-start = ((), (), s32[]{:S(2)}) async-start(), calls=%async_computation.16 | async-start | bytes 2949120 | tf_op jit(solution)/shard_map/all_gather | solution.py:30
  248.4 110.9 %reduce-scatter.20.cloned.1.call-start = ((), (), s32[]{:S(2)}) async-start(), calls=%async_computation.17 | async-start | bytes 2949120 | tf_op jit(solution)/shard_map/reduce_scatter | solution.py:34
  312.3 100.2 %all-gather.26.cloned.1.call-start = ((), (), s32[]{:S(2)}) async-start(), calls=%async_computation.18 | async-start | bytes 2949120 | tf_op jit(solution)/shard_map/all_gather | solution.py:30
  362.3 128.2 %reduce-scatter.22.cloned.1.call-start = ((), (), s32[]{:S(2)}) async-start(), calls=%async_computation.19 | async-start | bytes 2949120 | tf_op jit(solution)/shard_map/reduce_scatter | solution.py:34
  443.5 101.3 %all-gather.28.cloned.1.call-start = ((), (), s32[]{:S(2)}) async-start(), calls=%async_computation.20 | async-start | bytes 2949120 | tf_op jit(solution)/shard_map/all_gather | solution.py:30
  494.7 101.5 %all-gather.16.cloned.1.call-start = ((), (), s32[]{:S(2)}) async-start(), calls=%async_computation.11 | async-start | bytes 2949120 | tf_op jit(solution)/shard_map/all_gather | solution.py:30
  495.3 164.5 %reduce-scatter.24.cloned.1.call-start = ((), (), s32[]{:S(2)}) async-start(), calls=%async_computation.21 | async-start | bytes 2949120 | tf_op jit(solution)/shard_map/reduce_scatter | solution.py:34
  612.8 102.2 %all-gather.30.cloned.1.call-start = ((), (), s32[]{:S(2)}) async-start(), calls=%async_computation.22 | async-start | bytes 2949120 | tf_op jit(solution)/shard_map/all_gather | solution.py:30
  664.9 124.0 %reduce-scatter.26.cloned.1.call-start = ((), (), s32[]{:S(2)}) async-start(), calls=%async_computation.23 | async-start | bytes 2949120 | tf_op jit(solution)/shard_map/reduce_scatter | solution.py:34
  741.8 103.7 %all-gather.32.cloned.1.call-start = ((), (), s32[]{:S(2)}) async-start(), calls=%async_computation.24 | async-start | bytes 2949120 | tf_op jit(solution)/shard_map/all_gather | solution.py:30
  795.4 113.8 %reduce-scatter.28.cloned.1.call-start = ((), (), s32[]{:S(2)}) async-start(), calls=%async_computation.25 | async-start | bytes 2949120 | tf_op jit(solution)/shard_map/reduce_scatter | solution.py:34
  862.2 103.0 %all-gather.34.cloned.1.call-start = ((), (), s32[]{:S(2)}) async-start(), calls=%async_computation.26 | async-start | bytes 2949120 | tf_op jit(solution)/shard_map/all_gather | solution.py:30
  915.0 124.0 %reduce-scatter.30.cloned.1.call-start = ((), (), s32[]{:S(2)}) async-start(), calls=%async_computation.27 | async-start | bytes 2949120 | tf_op jit(solution)/shard_map/reduce_scatter | solution.py:34
  992.0 97.3 %reduce-scatter.32.cloned.1.call-start = ((), (), s32[]{:S(2)}) async-start(), calls=%async_computation.28 | async-start | bytes 2949120 | tf_op jit(solution)/shard_map/reduce_scatter | solution.py:34
  1001.3 160.8 %reduce-scatter.34.cloned.1.call-start = ((), (), s32[]{:S(2)}) async-start(), calls=%async_computation.30 | async-start | bytes 4423680
  1027.4 148.2 %collective-permute-start.6 = (bf16[1152,2304]{0,1:T(8,128)(2,1)}, bf16[1152,2304]{0,1:T(8,128)(2,1)}, u32[]{:S(2)}, u32[]{:S(2)}) collective-permute-start(bf16[1152,2304]{0,1:T(8,128)(2,1)} %broadcast_select_fusion), channel_id=1, source_target_pairs={{0,16},{16,0},{1,17},{17,1},{2,18},{18,2},{3,19},{19,3},{4,20},{20... | collective-permute-start | bytes 15925256 | tf_op jit(solution)/shard_map/ppermute | solution.py:188
  1096.1 201.0 %all-reduce.3.cloned.1.call-start = ((), (), s32[]{:S(2)}) async-start(), calls=%async_computation.29 | async-start | bytes 335872 | tf_op jit(solution)/shard_map/psum | solution.py:306
  1175.5 188.6 %reduce-scatter.38.cloned.1.call-start = ((), (), s32[]{:S(2)}) async-start(), calls=%async_computation.32 | async-start | bytes 6635520
  1193.4 213.6 %reduce-scatter.36.cloned.1.call-start = ((), (), s32[]{:S(2)}) async-start(), calls=%async_computation.31 | async-start | bytes 3317760
  1223.2 79.4 %collective-permute-start.4 = (f32[256,1152]{1,0:T(8,128)}, f32[256,1152]{1,0:T(8,128)}, u32[]{:S(2)}, u32[]{:S(2)}) collective-permute-start(f32[256,1152]{1,0:T(8,128)} %get-tuple-element.92), channel_id=1, source_target_pairs={{0,16},{16,0},{1,17},{17,1},{2,18},{18,2},{3,19},{19,3},{4,20},{20... | collective-permute-start | bytes 3538952 | tf_op jit(solution)/shard_map/ppermute | solution.py:188
  (111 other events, 1624.5 us)
Sparse Core Ops, SparseCore 0:
  11.2 43.5 all-gather.21
  80.0 50.0 all-gather.19
  132.5 60.7 all-gather.17
  196.1 48.0 reduce-scatter.17
  248.5 49.9 all-gather.23
  312.4 46.8 reduce-scatter.19
  362.4 49.9 all-gather.25
  443.6 46.8 reduce-scatter.21
  494.8 49.9 all-gather.27
  546.9 49.2 all-gather.15
  613.0 46.8 reduce-scatter.23
  665.0 49.9 all-gather.29
  742.0 46.8 reduce-scatter.25
  795.6 49.9 all-gather.31
  862.3 46.8 reduce-scatter.27
  915.1 49.9 all-gather.33
  992.1 46.8 reduce-scatter.29
  1041.7 47.5 reduce-scatter.31
  1096.2 65.8 reduce-scatter.33
  1175.7 121.3 all-reduce.2
  1300.1 63.9 reduce-scatter.37
  1367.1 39.8 reduce-scatter.35

commit v2 on v1

--- a/solution.py
+++ b/solution.py
@@ -1,8 +1,12 @@
+import functools
 import math
 
 import jax
 import jax.numpy as jnp
 from jax import lax
+from jax.experimental import pallas as pl
+from jax.experimental.pallas import tpu as pltpu
+from jax.sharding import Mesh
 from jax.sharding import PartitionSpec as P
 
 HD = 72
@@ -26,14 +30,158 @@
     return jax.nn.gelu(values, approximate=True)
 
 
+MESH = pl.DeviceIdType.MESH
+CHUNKS = 2
+
+
+def greet(nz, side, place):
+    barrier = pltpu.get_barrier_semaphore()
+    pl.semaphore_signal(barrier, inc=1, device_id={"section": 1 - side}, device_id_type=MESH)
+    for j in range(1, nz):
+        pl.semaphore_signal(
+            barrier, inc=1, device_id={"zl": lax.rem(place + j, nz)}, device_id_type=MESH
+        )
+    pl.semaphore_wait(barrier, nz)
+
+
+def push(src, dst, send, recv, target):
+    return pltpu.make_async_remote_copy(
+        src_ref=src, dst_ref=dst, send_sem=send, recv_sem=recv,
+        device_id=target, device_id_type=MESH,
+    )
+
+
+def spread_kernel(nz, x_ref, out_ref, local, send_c, recv_c, send_z, recv_z, send_f, recv_f):
+    side = lax.axis_index("section")
+    place = lax.axis_index("zl")
+    own = side * nz + place
+    step = x_ref.shape[0] // CHUNKS
+    greet(nz, side, place)
+    along = []
+    for c in range(CHUNKS):
+        rows = pl.ds(c * step, step)
+        for j in range(1, nz):
+            copy = push(
+                x_ref.at[rows], out_ref.at[own, rows], send_z.at[c, j - 1], recv_z.at[c, j - 1],
+                {"zl": lax.rem(place + j, nz)},
+            )
+            copy.start()
+            along.append(copy)
+    across = push(x_ref, out_ref.at[own], send_c, recv_c, {"section": 1 - side})
+    across.start()
+    kept = pltpu.make_async_copy(x_ref, out_ref.at[own], local)
+    kept.start()
+    handed = []
+    for c in range(CHUNKS):
+        rows = pl.ds(c * step, step)
+        for j in range(1, nz):
+            along[c * (nz - 1) + j - 1].wait_recv()
+            came = side * nz + lax.rem(place - j + nz, nz)
+            copy = push(
+                out_ref.at[came, rows], out_ref.at[came, rows],
+                send_f.at[c, j - 1], recv_f.at[c, j - 1], {"section": 1 - side},
+            )
+            copy.start()
+            handed.append(copy)
+    kept.wait()
+    across.wait()
+    for copy in along:
+        copy.wait_send()
+    for copy in handed:
+        copy.wait()
+
+
 def spread(values):
-    return lax.all_gather(values, "tensor", axis=0, tiled=True)
+    nz = lax.axis_size("zl")
+    many = (CHUNKS, nz - 1)
+    dma = pltpu.SemaphoreType.DMA
+    gathered = pl.pallas_call(
+        functools.partial(spread_kernel, nz),
+        out_shape=jax.ShapeDtypeStruct((2 * nz,) + values.shape, values.dtype),
+        in_specs=[pl.BlockSpec(memory_space=pl.ANY)],
+        out_specs=pl.BlockSpec(memory_space=pl.ANY),
+        scratch_shapes=[dma, dma, dma, dma(many), dma(many), dma(many), dma(many)],
+        compiler_params=pltpu.CompilerParams(collective_id=0, has_side_effects=True),
+        name="spread_tokens",
+    )(values)
+    return gathered.reshape(-1, values.shape[1])
+
+
+def collect_kernel(
+    nz, x_ref, out_ref, core_buf, mid_buf, z_buf, send_c, recv_c, send_z, recv_z
+):
+    side = lax.axis_index("section")
+    place = lax.axis_index("zl")
+    step = x_ref.shape[1] // CHUNKS
+    greet(nz, side, place)
+    across = {}
+    for j in list(range(1, nz)) + [0]:
+        there = lax.rem(place + j, nz)
+        for c in range(CHUNKS):
+            rows = pl.ds(c * step, step)
+            copy = push(
+                x_ref.at[(1 - side) * nz + there, rows], core_buf.at[j, rows],
+                send_c.at[c, j], recv_c.at[c, j], {"section": 1 - side},
+            )
+            copy.start()
+            across[c, j] = copy
+    along = {}
+    for j in range(1, nz):
+        there = lax.rem(place + j, nz)
+        for c in range(CHUNKS):
+            rows = pl.ds(c * step, step)
+            across[c, j].wait_recv()
+            mid_buf[j - 1, rows] = (
+                x_ref[side * nz + there, rows].astype(jnp.float32)
+                + core_buf[j, rows].astype(jnp.float32)
+            ).astype(jnp.bfloat16)
+            copy = push(
+                mid_buf.at[j - 1, rows], z_buf.at[j - 1, rows],
+                send_z.at[c, j - 1], recv_z.at[c, j - 1], {"zl": there},
+            )
+            copy.start()
+            along[c, j] = copy
+    for c in range(CHUNKS):
+        rows = pl.ds(c * step, step)
+        across[c, 0].wait_recv()
+        total = x_ref[side * nz + place, rows].astype(jnp.float32) + core_buf[0, rows].astype(
+            jnp.float32
+        )
+        for j in range(1, nz):
+            along[c, j].wait_recv()
+            total = total + z_buf[j - 1, rows].astype(jnp.float32)
+        out_ref[rows] = total
+    for copy in across.values():
+        copy.wait_send()
+    for copy in along.values():
+        copy.wait_send()
 
 
 def collect(values):
-    return lax.psum_scatter(
-        values.astype(jnp.bfloat16), "tensor", scatter_dimension=0, tiled=True
-    ).astype(jnp.float32)
+    nz = lax.axis_size("zl")
+    width = values.shape[1]
+    rows = values.shape[0] // (2 * nz)
+    dma = pltpu.SemaphoreType.DMA
+    vmem = pl.BlockSpec(memory_space=pltpu.VMEM)
+    return pl.pallas_call(
+        functools.partial(collect_kernel, nz),
+        out_shape=jax.ShapeDtypeStruct((rows, width), jnp.float32),
+        in_specs=[vmem],
+        out_specs=vmem,
+        scratch_shapes=[
+            pltpu.VMEM((nz, rows, width), jnp.bfloat16),
+            pltpu.VMEM((nz - 1, rows, width), jnp.bfloat16),
+            pltpu.VMEM((nz - 1, rows, width), jnp.bfloat16),
+            dma((CHUNKS, nz)),
+            dma((CHUNKS, nz)),
+            dma((CHUNKS, nz - 1)),
+            dma((CHUNKS, nz - 1)),
+        ],
+        compiler_params=pltpu.CompilerParams(
+            collective_id=1, has_side_effects=True, vmem_limit_bytes=24 * 2**20
+        ),
+        name="collect_tokens",
+    )(values.astype(jnp.bfloat16).reshape(2 * nz, rows, width))
 
 
 def mm(left, right, left_dim, right_dim):
@@ -81,7 +229,11 @@
     return outputs, stored
 
 
-def backward(upstream, stored, modulation, w_attn, w_mlp):
+def scatter_dp(grads):
+    return lax.psum_scatter(grads, "dp", scatter_dimension=0, tiled=True)
+
+
+def backward(upstream, stored, modulation, w_attn, w_mlp, before):
     (
         norm_in, inv_in, normed, queries, keys, values, probs, attended, attended_rows,
         branch_attn, norm_mid, inv_mid, normed_mlp, hidden_pre, hidden, branch_mlp,
@@ -105,6 +257,9 @@
         ],
         axis=1,
     )
+    if before is not None:
+        grad_normed, before = lax.optimization_barrier((grad_normed, before))
+    mlp_grads = scatter_dp(mlp_grads)
     grad_shift_mlp = jnp.sum(grad_normed, axis=0)
     grad_scale_mlp = jnp.sum(grad_normed * norm_mid, axis=0)
     grad_middle = upstream + norm_back(norm_mid, inv_mid, grad_normed * (1.0 + scale_mlp))
@@ -145,6 +300,8 @@
         ],
         axis=1,
     )
+    grad_normed, mlp_grads = lax.optimization_barrier((grad_normed, mlp_grads))
+    attn_grads = scatter_dp(attn_grads)
     grad_shift_attn = jnp.sum(grad_normed, axis=0)
     grad_scale_attn = jnp.sum(grad_normed * norm_in, axis=0)
     grad_inputs = grad_middle + norm_back(norm_in, inv_in, grad_normed * (1.0 + scale_attn))
@@ -155,7 +312,7 @@
         ]
     )
     bias_grads = (bias_qkv[:cols], bias_qkv[2 * cols :], bias_out, bias_up, bias_down)
-    return grad_inputs, attn_grads, mlp_grads, bias_grads, mod_terms
+    return grad_inputs, attn_grads, mlp_grads, bias_grads, mod_terms, before
 
 
 def on_device(
@@ -173,7 +330,11 @@
     adaln_bias,
 ):
     section_rank = lax.axis_index("section")
-    tensor_rank = lax.axis_index("tensor")
+    half_rank = lax.axis_index("zh")
+    halves = lax.axis_size("zl")
+    tensor_rank = half_rank * halves + lax.axis_index("zl")
+    part_rank = section_rank * halves + lax.axis_index("zl")
+    at_home = section_rank == half_rank
     dp_rank = lax.axis_index("dp")
     is_first = section_rank == 0
     width = stack_ends.shape[3]
@@ -190,10 +351,21 @@
     def by_block(own, other):
         return (jnp.where(is_first, own, other), jnp.where(is_first, other, own))
 
-    own_ends = stack_ends[0]
-    mine = lax.dynamic_index_in_dim(own_ends, section_rank, 0, keepdims=False)
-    theirs = swap(lax.dynamic_index_in_dim(own_ends, 1 - section_rank, 0, keepdims=False))
-    inputs, cotangent = by_block(mine, theirs)
+    def bring(own):
+        pair = jnp.stack(by_block(own, swap(own)))
+        return pair, lax.ppermute(pair, ("section", "zh"), [(0, 1), (3, 2)])
+
+    def fetch(own):
+        pair, moved = bring(own)
+        return jnp.where(at_home, pair, moved)
+
+    ends = jnp.stack(by_block(stack_ends[0], swap(stack_ends[0])))
+    mine = lax.dynamic_index_in_dim(ends, half_rank, 1, keepdims=False)
+    theirs = lax.ppermute(
+        lax.dynamic_index_in_dim(ends, 1 - half_rank, 1, keepdims=False),
+        ("section", "zh"), [(0, 1), (3, 2)],
+    )
+    inputs, cotangent = jnp.where(at_home, mine, theirs)
 
     cond_all = lax.all_gather(cond, "dp", axis=0, tiled=True).astype(jnp.float32)
     silu_all = jax.nn.silu(cond_all).astype(jnp.bfloat16)
@@ -201,19 +373,19 @@
     mod_part = lax.psum_scatter(
         mm(silu_rows, adaln_weight[0], 1, 0), "dp", scatter_dimension=0, tiled=True
     )
-    mod_all = lax.all_gather(mod_part, ("section", "tensor"), axis=0)
-    mod_own = lax.dynamic_index_in_dim(mod_all, section_rank, 1, keepdims=False)
+    mod_all = lax.all_gather(mod_part, ("section", "zh", "zl"), axis=0)
+    mod_own = lax.dynamic_index_in_dim(mod_all, half_rank, 1, keepdims=False)
     mod_own = mod_own.reshape(2, -1)
 
-    attn_own = lax.all_gather(
-        jnp.concatenate([qkv_weight[0].reshape(depth, 3 * cols), out_weight[0].T], axis=1),
-        "dp", axis=0, tiled=True,
-    )
-    attn_blocks = by_block(attn_own, swap(attn_own))
-    mlp_own = lax.all_gather(
-        jnp.concatenate([up_weight[0], down_weight[0].T], axis=1), "dp", axis=0, tiled=True
-    )
-    mlp_blocks = by_block(mlp_own, swap(mlp_own))
+    attn_pair = fetch(
+        jnp.concatenate([qkv_weight[0].reshape(depth, 3 * cols), out_weight[0].T], axis=1)
+    )
+    mlp_pair = fetch(jnp.concatenate([up_weight[0], down_weight[0].T], axis=1))
+    attn_blocks = []
+    mlp_blocks = []
+    for block in range(2):
+        attn_blocks.append(lax.all_gather(attn_pair[block], "dp", axis=0, tiled=True))
+        mlp_blocks.append(lax.all_gather(mlp_pair[block], "dp", axis=0, tiled=True))
 
     bias_flat = jnp.concatenate(
         [qv_bias[0].reshape(-1), out_bias[0], up_bias[0], down_bias[0], adaln_bias[0]]
@@ -232,7 +404,7 @@
         ]
 
         def cut(vector, size):
-            return lax.dynamic_slice_in_dim(vector, tensor_rank * size, size, 0)
+            return lax.dynamic_slice_in_dim(vector, part_rank * size, size, 0)
 
         b_qkv = jnp.concatenate(
             [cut(parts[0], cols), jnp.zeros((cols,), jnp.float32), cut(parts[1], cols)]
@@ -249,33 +421,47 @@
         boundary, modulations[1], attn_blocks[1], mlp_blocks[1], biases[1]
     )
     back_last = backward(
-        cotangent.astype(jnp.float32), stored_last, modulations[1], attn_blocks[1], mlp_blocks[1]
+        cotangent.astype(jnp.float32), stored_last, modulations[1], attn_blocks[1], mlp_blocks[1], None
     )
     upstream = back_last[0].astype(jnp.bfloat16).astype(jnp.float32)
     back_first = backward(
-        upstream, stored_first, modulations[0], attn_blocks[0], mlp_blocks[0]
-    )
+        upstream, stored_first, modulations[0], attn_blocks[0], mlp_blocks[0], back_last[1]
+    )
+    back_last = (back_last[0], back_first[5]) + back_last[2:]
     backs = (back_first, back_last)
 
     def settle(which):
-        kept = jnp.where(is_first, backs[0][which], backs[1][which])
-        sent = swap(jnp.where(is_first, backs[1][which], backs[0][which]))
-        total = (kept.astype(jnp.float32) + sent.astype(jnp.float32)).astype(jnp.bfloat16)
-        return lax.psum_scatter(total, "dp", scatter_dimension=0, tiled=True).astype(jnp.float32)
+        pair = jnp.stack([back[which] for back in backs])
+        moved = lax.ppermute(pair, ("section", "zh"), [(1, 0), (2, 3)])
+        total = pair.astype(jnp.float32) + moved.astype(jnp.float32)
+        kept = lax.dynamic_index_in_dim(total, section_rank, 0, keepdims=False)
+        sent = lax.dynamic_index_in_dim(total, 1 - section_rank, 0, keepdims=False)
+        sent = swap(sent.astype(jnp.bfloat16)).astype(jnp.float32)
+        return jnp.where(at_home, kept, sent)
 
     mlp_total = settle(2)
     attn_total = settle(1)
 
-    first_end, last_end = back_first[0], outputs
-    kept = jnp.where(is_first, first_end, last_end)
-    sent = swap(jnp.where(is_first, last_end, first_end))
-    result_ends = jnp.stack(by_block(kept, sent))[None]
-
+    ends = jnp.stack([back_first[0], outputs])
+    moved = lax.ppermute(ends.astype(jnp.bfloat16), ("section", "zh"), [(1, 0), (2, 3)])
+    moved = moved.astype(jnp.float32)
+    latents = [
+        jnp.where(half_rank == lat, ends, moved)
+        for lat in range(2)
+    ]
+    ends = jnp.stack(latents, axis=1)
+    kept = lax.dynamic_index_in_dim(ends, section_rank, 0, keepdims=False)
+    sent = swap(lax.dynamic_index_in_dim(ends, 1 - section_rank, 0, keepdims=False))
+    result_ends = jnp.where(at_home, kept, sent)[None]
+
+    mod_terms = jnp.stack([backs[0][4], backs[1][4]])
+    mod_terms = jnp.stack(
+        [jnp.where(half_rank == lat, mod_terms, 0.0) for lat in range(2)]
+    ).reshape(2, -1, mod_cols).transpose(1, 0, 2)
     mod_terms = lax.psum_scatter(
-        jnp.stack([backs[0][4], backs[1][4]]), "tensor", scatter_dimension=1, tiled=True
-    )
-    mod_grads = lax.all_gather(mod_terms, ("dp", "section"), axis=0)
-    mod_grads = lax.dynamic_index_in_dim(mod_grads, section_rank, 1, keepdims=False)
+        mod_terms.reshape(-1, 2 * mod_cols), ("section", "zh", "zl"), scatter_dimension=0, tiled=True
+    ).reshape(2, mod_cols)
+    mod_grads = lax.all_gather(mod_terms, "dp", axis=0, tiled=True)
     mod_grads = mod_grads.astype(jnp.bfloat16)
     grad_ada = mm(silu_rows, mod_grads, 0, 0)
     bias_ada = jnp.sum(mod_grads.astype(jnp.float32), axis=0)
@@ -291,10 +477,10 @@
         bias_q, bias_v, bias_out, bias_up, bias_down = backs[block][3]
         share = jnp.where((section_rank == block) & (dp_rank == 0), bias_ada, 0.0)
         pieces += [
-            place(bias_q, width, tensor_rank),
-            place(bias_v, width, tensor_rank),
+            place(bias_q, width, part_rank),
+            place(bias_v, width, part_rank),
             bias_out,
-            place(bias_up, sizes[3], tensor_rank),
+            place(bias_up, sizes[3], part_rank),
             bias_down,
             place(share, sizes[5], tensor_rank),
         ]
@@ -303,7 +489,7 @@
             jnp.zeros((lat_all, width), jnp.float32), grad_silu, dp_rank * depth, 1
         ).reshape(-1)
     )
-    summed = lax.psum(jnp.concatenate(pieces), ("section", "dp", "tensor"))
+    summed = lax.psum(jnp.concatenate(pieces), ("section", "dp", "zh", "zl"))
     per_block = marks[-1]
     bias_sums = jnp.where(is_first, summed[:per_block], summed[per_block : 2 * per_block])
     silu_total = summed[2 * per_block :].reshape(lat_all, width)
@@ -327,14 +513,16 @@
 
 
 def solution(mesh):
+    section, dp, tensor = mesh.devices.shape
+    fine = Mesh(mesh.devices.reshape(section, dp, 2, tensor // 2), ("section", "dp", "zh", "zl"))
     in_specs = (
-        P("section", "dp", "tensor", None),
+        P("section", "dp", ("zh", "zl"), None),
         P("dp", None),
-        P("section", "dp", None, "tensor"),
-        P("section", "tensor", "dp"),
-        P("section", "dp", "tensor"),
-        P("section", "tensor", "dp"),
-        P("section", "dp", "tensor"),
+        P("section", "dp", None, ("zh", "zl")),
+        P("section", ("zh", "zl"), "dp"),
+        P("section", "dp", ("zh", "zl")),
+        P("section", ("zh", "zl"), "dp"),
+        P("section", "dp", ("zh", "zl")),
         P("section", None, None),
         P("section", None),
         P("section", None),
@@ -342,13 +530,13 @@
         P("section", None),
     )
     out_specs = (
-        P("section", "dp", "tensor", None),
+        P("section", "dp", ("zh", "zl"), None),
         P("dp", None),
-        P("section", "dp", None, "tensor"),
-        P("section", "tensor", "dp"),
-        P("section", "dp", "tensor"),
-        P("section", "tensor", "dp"),
-        P("section", "dp", "tensor"),
+        P("section", "dp", None, ("zh", "zl")),
+        P("section", ("zh", "zl"), "dp"),
+        P("section", "dp", ("zh", "zl")),
+        P("section", ("zh", "zl"), "dp"),
+        P("section", "dp", ("zh", "zl")),
         P("section", None, None),
         P("section", None),
         P("section", None),
@@ -356,5 +544,5 @@
         P("section", None),
     )
     return jax.shard_map(
-        on_device, mesh=mesh, in_specs=in_specs, out_specs=out_specs, check_vma=False
-    )
+        on_device, mesh=fine, in_specs=in_specs, out_specs=out_specs, check_vma=False
+    )

time: 1430 us -> 1180 us (0.83)
  waiting for transfers between devices: 967 us -> 312 us
  Pallas kernels: 0 us -> 325 us
  starting transfers between devices: 5.01 us -> 63.2 us
  local copies, waits for them, and re-layouts: 91.6 us -> 122 us
  other arithmetic: 102 us -> 87 us
    all_gather x10 -> x4, waiting for transfers between devices: 401 us -> 0.08 us  [the longest x2 0.04 us: on_device(): mlp_blocks.append(lax.all_gather(mlp_pair[block], 'dp', axis=0, tiled=True))]
    reduce_scatter x8 -> x1, waiting for transfers between devices: 329 us -> 0.02 us  [scatter_dp(): return lax.psum_scatter(grads, 'dp', scatter_dimension=0, tiled=True)]
    pallas_call x0 -> x16, Pallas kernels: none -> 325 us  [the longest x8 172 us: spread(): pl.pallas_call(functools.partial(spread_kernel, nz), out_shape=jax.ShapeD...]
    psum x1, waiting for transfers between devices: 70.9 us -> 116 us  [on_device(): summed = lax.psum(jnp.concatenate(pieces), ('section', 'dp', 'zh', 'zl'))]
    ppermute x7, starting transfers between devices: 1.68 us -> 43.6 us  [swap(): return lax.ppermute(value, 'section', SWAP)]
    ppermute x0 -> x6, waiting for transfers between devices: none -> 41.6 us  [the longest x2 28.4 us: bring(): return (pair, lax.ppermute(pair, ('section', 'zh'), [(0, 1), (3, 2)]))]
    ppermute x0 -> x6, starting transfers between devices: none -> 18.1 us  [the longest x2 9.83 us: bring(): return (pair, lax.ppermute(pair, ('section', 'zh'), [(0, 1), (3, 2)]))]
    select_n x3 -> x1, other arithmetic: 15.4 us -> 0.01 us  [by_block(): return (jnp.where(is_first, own, other), jnp.where(is_first, other, own))]
  transfers between devices with their start and end apart: 29 -> 23, of which waited for: 23 -> 7; matrix products, arithmetic and copies ran while one was open for 14% -> 21% of each run, Pallas kernels for 0% -> 20%
where the time goes in v2:
time: 1180 us; the launch traced here: 1160 us
  Pallas kernels  325 us (28%)
  waiting for transfers between devices  312 us (26%)
  matrix products  177 us (15%)
  local copies, waits for them, and re-layouts  122 us (10%)
  other arithmetic  87 us (7%)
  starting transfers between devices  63.2 us (5%)
  blocking collectives  57.4 us (5%)
  between operations  17.5 us (1%)
    pallas_call x8, Pallas kernels, spread(): pl.pallas_call(functools.partial(spread_kernel, nz), out_shape=jax.ShapeD...  172 us
    pallas_call x8, Pallas kernels, collect(): pl.pallas_call(functools.partial(collect_kernel, nz), out_shape=jax.Shape...  154 us
    unnamed x14, waiting for transfers between devices  154 us
    dot_general x27, matrix products, mm(): lax.dot_general(left, right, (((left_dim,), (right_dim,)), ((), ())), pre...  119 us
    psum x1, waiting for transfers between devices, on_device(): summed = lax.psum(jnp.concatenate(pieces), ('section', 'dp', 'zh', 'zl'))  116 us
    unnamed x262, local copies, waits for them, and re-layouts  69.8 us
    ppermute x7, starting transfers between devices, swap(): return lax.ppermute(value, 'section', SWAP)  43.6 us
    ppermute x2, waiting for transfers between devices, bring(): return (pair, lax.ppermute(pair, ('section', 'zh'), [(0, 1), (3, 2)]))  28.4 us
  transfers between devices with their start and end apart: 23, of which 7 were waited for; matrix products, arithmetic and copies ran while one was open for 21% of the time, Pallas kernels for 20%

profile of v2, /device:TPU:0, one launch (start us, length us, event | category | flops | bytes accessed | tf_op | source)
XLA Modules:
  0.0 1161.5 jit_solution(4465150145478122105)
XLA Ops:
  50.8 20.8 %collective-permute-done.4 = bf16[2,288,2304]{2,1,0:T(8,128)(2,1)} collective-permute-done((bf16[2,288,2304]{2,1,0:T(8,128)(2,1)}, bf16[2,288,2304]{2,1,0:T(8,128)(2,1)}, u32[]{:S(2)}, u32[]{:S(2)}) %collective-permute-start.4) | collective-permute-done | bytes 2654240 | tf_op jit(solution)/shard_map/ppermute | solution.py:356
  76.6 42.5 %collective-permute-start.2 = (bf16[16128]{0:T(1024)(128)(2,1)S(1)}, bf16[16128]{0:T(1024)(128)(2,1)S(1)}, u32[]{:S(2)}, u32[]{:S(2)}) collective-permute-start(bf16[16128]{0:T(1024)(128)(2,1)S(1)} %constant_dynamic-update-slice_fusion.7), channel_id=1, source_target_pairs={{0,16},{16,0},{1,17},{17,1},{2,18},{18,2},{3,19},{19,3},{4,20},{20... | collective-permute-start | bytes 96776 | tf_op jit(solution)/shard_map/ppermute | solution.py:349
  129.8 16.4 %all-reduce = f32[8,1728]{1,0:T(8,128)S(1)} all-reduce(f32[8,1728]{1,0:T(8,128)S(1)} %fusion.107), channel_id=7, replica_groups=mesh['section'=2,'dp'=4,'zh'=2,'zl'=2] {'dp'}, use_global_device_ids=true, to_apply=%region_0.1.clone | all-reduce | flops 13824 | bytes 110592
  146.3 23.9 %all-gather.6 = f32[8,2,1728]{2,1,0:T(2,128)S(1)} all-gather(f32[1,2,1728]{2,1,0:T(2,128)S(1)} %dynamic-slice_bitcast_fusion), channel_id=2, replica_groups=mesh['section'=2,'dp'=4,'zh'=2,'zl'=2] {'section','zh','zl'}, dimensions={0}, use_global_device_ids=true | all-gather | bytes 124416 | tf_op jit(solution)/shard_map/all_gather | solution.py:376
  178.8 13.1 %collective-permute-done.1 = bf16[2,256,1152]{2,1,0:T(8,128)(2,1)S(1)} collective-permute-done((bf16[2,256,1152]{2,1,0:T(8,128)(2,1)S(1)}, bf16[2,256,1152]{2,1,0:T(8,128)(2,1)S(1)}, u32[]{:S(2)}, u32[]{:S(2)}) %collective-permute-start.1) | collective-permute-done | bytes 1179680 | tf_op jit(solution)/shard_map/ppermute | solution.py:364
  194.6 33.1 %spread_tokens.9 = bf16[4,256,1152]{2,1,0:T(8,128)(2,1)} custom-call(bf16[256,1152]{1,0:T(8,128)(2,1)} %get-tuple-element.132.x_ref), custom_call_target="tpu_custom_call" | custom-call | tf_op jit(solution)/shard_map/spread_tokens/pallas_call | solution.py:98
  227.8 19.2 %spread_tokens.8 = bf16[4,256,1152]{2,1,0:T(8,128)(2,1)} custom-call(bf16[256,1152]{1,0:T(8,128)(2,1)} %get-tuple-element.92.x_ref), custom_call_target="tpu_custom_call" | custom-call | tf_op jit(solution)/shard_map/spread_tokens/pallas_call | solution.py:98
  276.8 17.4 %collect_tokens.8 = f32[256,1152]{1,0:T(8,128)S(1)} custom-call(bf16[4,256,1152]{2,1,0:T(8,128)(2,1)S(1)} %bitcast.262), custom_call_target="tpu_custom_call" | custom-call | tf_op jit(solution)/shard_map/collect_tokens/pallas_call | solution.py:166
  296.9 19.7 %spread_tokens.10 = bf16[4,256,1152]{2,1,0:T(8,128)(2,1)} custom-call(bf16[256,1152]{1,0:T(8,128)(2,1)} %add_convert_fusion.4.x_ref), custom_call_target="tpu_custom_call" | custom-call | tf_op jit(solution)/shard_map/spread_tokens/pallas_call | solution.py:98
  327.6 17.4 %collect_tokens.9 = f32[256,1152]{1,0:T(8,128)S(1)} custom-call(bf16[4,256,1152]{2,1,0:T(8,128)(2,1)S(1)} %bitcast.263), custom_call_target="tpu_custom_call" | custom-call | tf_op jit(solution)/shard_map/collect_tokens/pallas_call | solution.py:166
  347.2 19.3 %spread_tokens.11 = bf16[4,256,1152]{2,1,0:T(8,128)(2,1)} custom-call(bf16[256,1152]{1,0:T(8,128)(2,1)} %fusion.79.x_ref), custom_call_target="tpu_custom_call" | custom-call | tf_op jit(solution)/shard_map/spread_tokens/pallas_call | solution.py:98
  395.9 17.4 %collect_tokens.10 = f32[256,1152]{1,0:T(8,128)S(1)} custom-call(bf16[4,256,1152]{2,1,0:T(8,128)(2,1)S(1)} %bitcast.264), custom_call_target="tpu_custom_call" | custom-call | tf_op jit(solution)/shard_map/collect_tokens/pallas_call | solution.py:166
  415.7 19.5 %spread_tokens.12 = bf16[4,256,1152]{2,1,0:T(8,128)(2,1)} custom-call(bf16[256,1152]{1,0:T(8,128)(2,1)} %add_convert_fusion.2.x_ref), custom_call_target="tpu_custom_call" | custom-call | tf_op jit(solution)/shard_map/spread_tokens/pallas_call | solution.py:98
  453.4 17.4 %collect_tokens.11 = f32[256,1152]{1,0:T(8,128)S(1)} custom-call(bf16[4,256,1152]{2,1,0:T(8,128)(2,1)S(1)} %bitcast.265), custom_call_target="tpu_custom_call" | custom-call | tf_op jit(solution)/shard_map/collect_tokens/pallas_call | solution.py:166
  473.7 19.5 %spread_tokens.13 = bf16[4,256,1152]{2,1,0:T(8,128)(2,1)} custom-call(bf16[256,1152]{1,0:T(8,128)(2,1)} %get-tuple-element.94.x_ref), custom_call_target="tpu_custom_call" | custom-call | tf_op jit(solution)/shard_map/spread_tokens/pallas_call | solution.py:98
  556.4 17.4 %collect_tokens.12 = f32[256,1152]{1,0:T(8,128)S(1)} custom-call(bf16[4,256,1152]{2,1,0:T(8,128)(2,1)S(1)} %bitcast.259), custom_call_target="tpu_custom_call" | custom-call | tf_op jit(solution)/shard_map/collect_tokens/pallas_call | solution.py:166
  577.2 55.1 %reduce-scatter.13.cloned.1.call-done = bf16[288,2304]{1,0:T(8,128)(2,1)} async-done(((bf16[1152,2304]{1,0:T(8,128)(2,1)}), bf16[288,2304]{1,0:T(8,128)(2,1)}) %reduce-scatter.13.cloned.1.call-update) | async-done | bytes 1327120
  641.4 20.6 %spread_tokens.14 = bf16[4,256,1152]{2,1,0:T(8,128)(2,1)} custom-call(bf16[256,1152]{1,0:T(8,128)(2,1)} %get-tuple-element.101.x_ref), custom_call_target="tpu_custom_call" | custom-call | tf_op jit(solution)/shard_map/spread_tokens/pallas_call | solution.py:98
  679.0 16.4 %collect_tokens.13 = f32[256,1152]{1,0:T(8,128)S(1)} custom-call(bf16[4,256,1152]{2,1,0:T(8,128)(2,1)S(1)} %bitcast.260), custom_call_target="tpu_custom_call" | custom-call | tf_op jit(solution)/shard_map/collect_tokens/pallas_call | solution.py:166
  699.6 20.6 %spread_tokens.15 = bf16[4,256,1152]{2,1,0:T(8,128)(2,1)} custom-call(bf16[256,1152]{1,0:T(8,128)(2,1)} %get-tuple-element.103.x_ref), custom_call_target="tpu_custom_call" | custom-call | tf_op jit(solution)/shard_map/spread_tokens/pallas_call | solution.py:98
  783.5 16.7 %collect_tokens.15 = f32[256,1152]{1,0:T(8,128)S(1)} custom-call(bf16[4,256,1152]{2,1,0:T(8,128)(2,1)S(1)} %bitcast.258), custom_call_target="tpu_custom_call" | custom-call | tf_op jit(solution)/shard_map/collect_tokens/pallas_call | solution.py:166
  814.9 33.9 %collect_tokens.14 = f32[256,1152]{1,0:T(8,128)S(1)} custom-call(bf16[4,256,1152]{2,1,0:T(8,128)(2,1)S(1)} %bitcast.261), custom_call_target="tpu_custom_call" | custom-call | tf_op jit(solution)/shard_map/collect_tokens/pallas_call | solution.py:166
  897.3 98.4 %all-reduce.7.cloned.1.call-done = f32[8,3456]{1,0:T(8,128)} async-done(((f32[8,3456]{1,0:T(8,128)}), f32[8,3456]{1,0:T(8,128)}) %all-reduce.7.cloned.1.call-update) | async-done | bytes 110608
  1024.3 115.8 %all-reduce.5.cloned.1.call-done = f32[41472]{0:T(1024)} async-done(((f32[41472]{0:T(1024)}), f32[41472]{0:T(1024)}) %all-reduce.5.cloned.1.call-update) | async-done | bytes 165904 | tf_op jit(solution)/shard_map/psum | solution.py:492
  (517 shorter events, 432.7 us)
Async XLA Ops:
  7.2 240.3 %all-gather.15.cloned.1.call-start = ((), (), s32[]{:S(2)}) async-start(), calls=%async_computation.6 | async-start | bytes 3317760 | tf_op jit(solution)/shard_map/all_gather | solution.py:387
  11.0 2.8 collective-permute-start.5
  13.7 14.9 %collective-permute-start.3 = (bf16[288,2304]{1,0:T(8,128)(2,1)}, bf16[288,2304]{1,0:T(8,128)(2,1)}, u32[]{:S(2)}, u32[]{:S(2)}) collective-permute-start(bf16[288,2304]{1,0:T(8,128)(2,1)} %pad_maximum_fusion.10), channel_id=1, source_target_pairs={{0,16},{16,0},{1,17},{17,1},{2,18},{18,2},{3,19},{19,3},{4,20},{20... | collective-permute-start | bytes 3981320 | tf_op jit(solution)/shard_map/ppermute | solution.py:349
  21.6 21.5 %collective-permute-start.6 = (bf16[2,288,1152]{2,1,0:T(8,128)(2,1)}, bf16[2,288,1152]{2,1,0:T(8,128)(2,1)}, u32[]{:S(2)}, u32[]{:S(2)}) collective-permute-start(bf16[2,288,1152]{2,1,0:T(8,128)(2,1)} %copy.82), channel_id=1, source_target_pairs={{0,2},{18,16},{1,3},{19,17},{4,6},{22,20},{5,7},{23,21},{8,10},{26... | collective-permute-start | bytes 3981320 | tf_op jit(solution)/shard_map/ppermute | solution.py:356
  32.6 38.9 %collective-permute-start.4 = (bf16[2,288,2304]{2,1,0:T(8,128)(2,1)}, bf16[2,288,2304]{2,1,0:T(8,128)(2,1)}, u32[]{:S(2)}, u32[]{:S(2)}) collective-permute-start(bf16[2,288,2304]{2,1,0:T(8,128)(2,1)} %pad_maximum_fusion.2), channel_id=1, source_target_pairs={{0,2},{18,16},{1,3},{19,17},{4,6},{22,20},{5,7},{23,21},{8,10},{26... | collective-permute-start | bytes 7962632 | tf_op jit(solution)/shard_map/ppermute | solution.py:356
  50.8 265.9 %all-gather.17.cloned.1.call-start = ((), (), s32[]{:S(2)}) async-start(), calls=%async_computation.7 | async-start | bytes 6635520 | tf_op jit(solution)/shard_map/all_gather | solution.py:388
  75.0 291.5 %all-gather.19.cloned.1.call-start = ((), (), s32[]{:S(2)}) async-start(), calls=%async_computation.8 | async-start | bytes 3317760 | tf_op jit(solution)/shard_map/all_gather | solution.py:387
  76.6 93.9 %collective-permute-start.2 = (bf16[16128]{0:T(1024)(128)(2,1)S(1)}, bf16[16128]{0:T(1024)(128)(2,1)S(1)}, u32[]{:S(2)}, u32[]{:S(2)}) collective-permute-start(bf16[16128]{0:T(1024)(128)(2,1)S(1)} %constant_dynamic-update-slice_fusion.7), channel_id=1, source_target_pairs={{0,16},{16,0},{1,17},{17,1},{2,18},{18,2},{3,19},{19,3},{4,20},{20... | collective-permute-start | bytes 96776 | tf_op jit(solution)/shard_map/ppermute | solution.py:349
  119.1 53.3 %collective-permute-start = (bf16[2,256,1152]{2,1,0:T(8,128)(2,1)S(1)}, bf16[2,256,1152]{2,1,0:T(8,128)(2,1)}, u32[]{:S(2)}, u32[]{:S(2)}) collective-permute-start(bf16[2,256,1152]{2,1,0:T(8,128)(2,1)S(1)} %bitcast.319), channel_id=1, source_target_pairs={{0,16},{16,0},{1,17},{17,1},{2,18},{18,2},{3,19},{19,3},{4,20},{20... | collective-permute-start | bytes 3538952 | tf_op jit(solution)/shard_map/ppermute | solution.py:349
  170.5 123.7 %copy-start.71 = (f32[1152]{0:T(1024)}, f32[1152]{0:T(1024)S(1)}, u32[]{:S(2)}) copy-start(f32[1152]{0:T(1024)S(1)} %get-tuple-element.144) | copy-start | bytes 13828
  171.7 263.5 %all-gather.13.cloned.1.call-start = ((), (), s32[]{:S(2)}) async-start(), calls=%async_computation.5 | async-start | bytes 6635520 | tf_op jit(solution)/shard_map/all_gather | solution.py:388
  174.0 18.0 %collective-permute-start.1 = (bf16[2,256,1152]{2,1,0:T(8,128)(2,1)S(1)}, bf16[2,256,1152]{2,1,0:T(8,128)(2,1)S(1)}, u32[]{:S(2)}, u32[]{:S(2)}) collective-permute-start(bf16[2,256,1152]{2,1,0:T(8,128)(2,1)S(1)} %fusion.101), channel_id=1, source_target_pairs={{0,2},{18,16},{1,3},{19,17},{4,6},{22,20},{5,7},{23,21},{8,10},{26... | collective-permute-start | bytes 3538952 | tf_op jit(solution)/shard_map/ppermute | solution.py:364
  247.0 327.8 %reduce-scatter.15.cloned.1.call-start = ((), (), s32[]{:S(2)}) async-start(), calls=%async_computation.10 | async-start | bytes 3317760
  527.1 105.2 %reduce-scatter.13.cloned.1.call-start = ((), (), s32[]{:S(2)}) async-start(), calls=%async_computation.9 | async-start | bytes 6635520
  551.3 254.5 %reduce-scatter.19.cloned.1.call-start = ((), (), s32[]{:S(2)}) async-start(), calls=%async_computation.12 | async-start | bytes 3317760 | tf_op jit(solution)/shard_map/reduce_scatter | solution.py:233
  751.1 124.2 %reduce-scatter.17.cloned.1.call-start = ((), (), s32[]{:S(2)}) async-start(), calls=%async_computation.11 | async-start | bytes 6635520
  774.8 220.9 %all-reduce.7.cloned.1.call-start = ((), (), s32[]{:S(2)}) async-start(), calls=%async_computation.13 | async-start | bytes 221184
  808.5 50.8 %collective-permute-start.9 = (bf16[2,288,1152]{2,1,0:T(8,128)(2,1)}, bf16[2,288,1152]{2,1,0:T(8,128)(2,1)}, u32[]{:S(2)}, u32[]{:S(2)}) collective-permute-start(bf16[2,288,1152]{2,1,0:T(8,128)(2,1)} %pad_maximum_fusion.11), channel_id=1, source_target_pairs={{2,0},{16,18},{3,1},{17,19},{6,4},{20,22},{7,5},{21,23},{10,8},{24... | collective-permute-start | bytes 3981320 | tf_op jit(solution)/shard_map/ppermute | solution.py:435
  861.3 2.2 collective-permute-start.10
  881.5 138.3 %collective-permute-start.7 = (bf16[2,256,1152]{2,1,0:T(8,128)(2,1)S(1)}, bf16[2,256,1152]{2,1,0:T(8,128)(2,1)}, u32[]{:S(2)}, u32[]{:S(2)}) collective-permute-start(bf16[2,256,1152]{2,1,0:T(8,128)(2,1)S(1)} %fusion.58), channel_id=1, source_target_pairs={{2,0},{16,18},{3,1},{17,19},{6,4},{20,22},{7,5},{21,23},{10,8},{24... | collective-permute-start | bytes 3538952 | tf_op jit(solution)/shard_map/ppermute | solution.py:446
  890.3 249.8 %all-reduce.5.cloned.1.call-start = ((), (), s32[]{:S(2)}) async-start(), calls=%async_computation.4 | async-start | bytes 335872 | tf_op jit(solution)/shard_map/psum | solution.py:492
  896.0 247.1 %collective-permute-start.11 = (bf16[2,288,2304]{2,1,0:T(8,128)(2,1)}, bf16[2,288,2304]{2,1,0:T(8,128)(2,1)}, u32[]{:S(2)}, u32[]{:S(2)}) collective-permute-start(bf16[2,288,2304]{2,1,0:T(8,128)(2,1)} %pad_maximum_fusion.5), channel_id=1, source_target_pairs={{2,0},{16,18},{3,1},{17,19},{6,4},{20,22},{7,5},{21,23},{10,8},{24... | collective-permute-start | bytes 7962632 | tf_op jit(solution)/shard_map/ppermute | solution.py:435
  1024.3 126.3 %collective-permute-start.8 = (f32[2,256,1152]{2,1,0:T(8,128)}, f32[2,256,1152]{2,1,0:T(8,128)}, u32[]{:S(2)}, u32[]{:S(2)}) collective-permute-start(f32[2,256,1152]{2,1,0:T(8,128)} %fusion.27), channel_id=1, source_target_pairs={{0,16},{16,0},{1,17},{17,1},{2,18},{18,2},{3,19},{19,3},{4,20},{20... | collective-permute-start | bytes 7077896 | tf_op jit(solution)/shard_map/ppermute | solution.py:349
  1146.4 5.9 collective-permute-start.12
  (111 other events, 1722.2 us)
Sparse Core Ops, SparseCore 0:
  50.9 85.8 all-gather.14
  139.2 61.7 all-gather.16
  203.4 39.9 all-gather.18
  247.1 63.3 all-gather.12
  527.2 40.1 reduce-scatter.14
  570.3 61.9 reduce-scatter.12
  751.2 38.9 reduce-scatter.18
  793.2 62.0 reduce-scatter.16
  890.4 105.2 all-reduce.6
  1017.4 122.7 all-reduce.4
